TPU v7x, 128 devices: a whole 4x4x4 slice. The times are simulated.
128 devices in a mesh: gx: 8 (over z_hi, y), gy: 16 (over z_lo, x, core).
Axes of the slice: x: 4, y: 4, z: 4 (z_hi: 2, z_lo: 2; z = z_hi * 2 + z_lo), core: 2. Of those that a mesh axis runs over, the one named last changes fastest.
Arguments:
- wind_east: float32 [64, 256, 2048], P(None, 'gx', 'gy'), may hold values from -6 to 6
- wind_north: float32 [64, 256, 2048], P(None, 'gx', 'gy'), may hold values from -6 to 6
- pressure: float32 [64, 256, 2048], P(None, 'gx', 'gy'), may hold values from -6 to 6
- stiffness: float32 [256, 2048], P('gx', 'gy'), may hold values from 8 to 64
- parent_east: float32 [3, 64, 3, 2048], P(None, None, None, 'gy'), may hold values from -6 to 6
- parent_north: float32 [3, 64, 256, 3], P(None, None, 'gx'), may hold values from -6 to 6
- parent_corner: float32 [3, 64, 3, 3], replicated, may hold values from -6 to 6
- offsets: int32 [2], replicated, may hold values from 0 to 3, as said below
Outputs:
- moved_east: float32 [64, 256, 2048], P(None, 'gx', 'gy')
- moved_north: float32 [64, 256, 2048], P(None, 'gx', 'gy')
- moved_pressure: float32 [64, 256, 2048], P(None, 'gx', 'gy')
Inputs may be any that keep to these rules, and one draw needn't show every extreme that they name: At least one of the two offsets is 3.
All inputs are finite; a program needn't handle non-finite values.
Results may differ from a plain program's by a relative error of at most 0.00012.
Values sent between devices are 32-bit elements; how exact they have to be, the bound alone decides.
No kernel may reach another device: no remote copies, remote signals or barrier semaphores. Data moves between devices by JAX's collectives and lax.ppermute only.
A program may use at most 128 MiB of HBM per device.

v0:
```python
import functools

import jax
import jax.numpy as jnp
import numpy as np
from jax import lax
from jax.experimental import pallas as pl
from jax.experimental.pallas import tpu as pltpu
from jax.sharding import PartitionSpec as P

F32 = jnp.float32
BF16 = jnp.bfloat16

C1, C2, C3 = 0.45, 0.09, 0.01
CY = 0.01


def band():
    mat = np.zeros((256, 256), np.float32)
    for j in range(256):
        for k, w in ((1, 45.0), (2, -9.0), (3, 1.0)):
            mat[(j + k) % 256, j] = w
            mat[(j - k) % 256, j] = -w
    return mat


def swaps(count):
    inner = [(i, i ^ 1) for i in range(count)]
    outer = [(i, min(max(((i + 1) ^ 1) - 1, 0), count - 1)) for i in range(count)]
    return inner, outer


def lane_index():
    return lax.broadcasted_iota(jnp.int32, (1, 128), 1)


def roll_lanes(value, shift):
    return pltpu.roll(value, shift % 128, 1)


def dy(ext, mat):
    hi = ext.astype(BF16)
    lo = (ext - hi.astype(F32)).astype(BF16)
    return jnp.dot(hi, mat, preferred_element_type=F32) + jnp.dot(
        lo, mat, preferred_element_type=F32
    )


def pack(rows, width, step, lanes):
    out = None
    for m, row in enumerate(rows):
        moved = roll_lanes(row, m * step + width)
        out = moved if out is None else jnp.where(lanes >= m * step, moved, out)
    return out


def write_edges(buffers, east, first, second):
    def write(ref, side):
        at = 0
        for buf, width in buffers[side]:
            a = 0 if side == 0 else 8 - width
            for l in range(64):
                ref[at + width * l : at + width * (l + 1), :] = buf[l, a : a + width, :]
            at += 64 * width

    @pl.when(east)
    def _():
        write(first, 1)
        write(second, 0)

    @pl.when(jnp.logical_not(east))
    def _():
        write(first, 0)
        write(second, 1)


def x_edges_kernel(p, u, first, second, pw, pe, uw, ue, sems):
    copies = []
    for k, (src, buf, at) in enumerate(((p, pw, 0), (u, uw, 0), (p, pe, 24), (u, ue, 24))):
        copies.append(pltpu.make_async_copy(src.at[:, at : at + 8, :], buf, sems.at[k]))
    for copy in copies:
        copy.start()
    for copy in copies:
        copy.wait()
    even = lax.axis_index("gx") % 2 == 0
    write_edges((((pw, 6), (uw, 3)), ((pe, 6), (ue, 3))), even, first, second)


def y_edges_kernel(p, v, out):
    lanes = lane_index()
    for b in range(8):
        out[b] = pack([p[8 * b + m] for m in range(8)], 6, 16, lanes)
    for b in range(4):
        out[8 + b] = pack([v[16 * b + m] for m in range(16)], 3, 8, lanes)


def y_pack_kernel(p, out):
    lanes = lane_index()
    for b in range(8):
        out[b] = pack([p[8 * b + m] for m in range(8)], 6, 16, lanes)


def coefficients_kernel(s_ref, inv_ref, g_ref):
    s = s_ref[...]
    prev = None
    for l in range(64):
        if l == 0:
            div = 1.0 + s
        elif l < 63:
            div = 1.0 + 2.0 * s - s * prev
        else:
            div = 1.0 + s - s * prev
        inv = 1.0 / div
        inv_ref[l] = inv
        prev = s * inv
        g_ref[l] = prev


def difference(at):
    return C1 * (at(1) - at(-1)) - C2 * (at(2) - at(-2)) + C3 * (at(3) - at(-3))


def inner_kernel(first_step, p, u, v, *rest):
    if first_step:
        inv, g, mat, y1, y2, keep1, keep2, keep3, p_out, u_out, v_out, vh_out, rest_out, w_buf = rest
        du = 0
    else:
        vh_in, inv, g, mat, y1, y2, p_out, u_out, v_out, rest_out, w_buf = rest
        du = 8
    lanes = lane_index()
    gy = lax.axis_index("gy")
    even_y = gy % 2 == 0
    in_s = gy > 0
    in_n = gy < lax.axis_size("gy") - 1
    lane_ok = jnp.where(lanes < 64, jnp.where(in_n, 1.0, 0.0), jnp.where(in_s, 1.0, 0.0))

    def sides(b, low):
        a, c = y1[b], y2[b]
        north = jnp.where(in_n, jnp.where(even_y, a, c), 0.0)
        south = jnp.where(in_s, jnp.where(even_y, c, a), 0.0)
        return jnp.where(low, south, north)

    w = jnp.zeros((16, 128), F32)
    for b in range(8):
        blk = sides(b, lanes % 16 < 6)
        halo = jnp.concatenate([roll_lanes(blk, -(16 * m + 6)) for m in range(8)], axis=0)
        if first_step:
            blk = sides(8 + b // 2, lanes % 8 < 3)
            at = 64 * (b % 2) + 3
            vh = jnp.concatenate([roll_lanes(blk, -(at + 8 * m)) for m in range(8)], axis=0)
        else:
            vh = vh_in[8 * b : 8 * b + 8].reshape(256, 128)
        own = p[8 * b : 8 * b + 8].reshape(256, 128)
        d = dy(jnp.concatenate([own, halo], axis=1), mat[...])
        v1 = v[8 * b : 8 * b + 8].reshape(256, 128) - CY * d[:, :128]
        vh = (vh - CY * d[:, 128:]) * lane_ok
        v_out[8 * b : 8 * b + 8] = v1.reshape(8, 32, 128)
        if first_step:
            vh_out[8 * b : 8 * b + 8] = vh.reshape(8, 32, 128)
        d2 = dy(jnp.concatenate([v1, vh], axis=1), mat[:, :128])
        left = own - CY * d2
        for m in range(8):
            l = 8 * b + m
            row = left[32 * m : 32 * m + 32]
            rest_out[l, 0:8, :] = row[0:8]
            rest_out[l, 8:16, :] = row[24:32]
            step = difference(lambda k: p[l, 5 + k : 29 + k, :])
            u_out[l, 13:37, :] = u[l, du + 5 : du + 29, :] - step
            rhs = row[8:24] - difference(lambda k: u_out[l, 16 + k : 32 + k, :])
            w = rhs * inv[l, 8:24, :] + g[l, 8:24, :] * w
            w_buf[l] = w
    q = jnp.zeros((16, 128), F32)
    for l in range(63, -1, -1):
        q = w_buf[l] + g[l, 8:24, :] * q
        p_out[l, 8:24, :] = q


def outer_kernel(first_step, x1, x2, p, u, inv, g, rest, p_in, u_in, *tail):
    if first_step:
        p_out, u_out, first, second, pw, pe, uw, ue, w_buf = tail
    else:
        v, pn, p_out, u_out, east, pw, pe, w_buf = tail
    gx = lax.axis_index("gx")
    even = gx % 2 == 0
    in_w = gx > 0
    in_e = gx < lax.axis_size("gx") - 1

    def fill(ref, west):
        for l in range(64):
            part = jnp.where(in_w if west else in_e, ref[6 * l : 6 * l + 6, :], 0.0)
            if west:
                pw[l, 2:8, :] = part
            else:
                pe[l, 8:14, :] = part
            if first_step:
                part = ref[384 + 3 * l : 387 + 3 * l, :]
                if west:
                    uw[l, 5:8, :] = part
                else:
                    ue[l, 8:11, :] = part

    @pl.when(even)
    def _():
        fill(x1, False)
        fill(x2, True)

    @pl.when(jnp.logical_not(even))
    def _():
        fill(x1, True)
        fill(x2, False)

    rows = lax.broadcasted_iota(jnp.int32, (8, 128), 0)
    ok_w = jnp.where(rows < 3, jnp.where(in_w, 1.0, 0.0), 1.0)
    ok_e = jnp.where(rows >= 3, jnp.where(in_e, 1.0, 0.0), 1.0)
    w = jnp.zeros((16, 128), F32)
    for l in range(64):
        pw[l, 8:16, :] = p[l, 0:8, :]
        pe[l, 0:8, :] = p[l, 24:32, :]
        if first_step:
            uw[l, 8:16, :] = u[l, 0:8, :]
            ue[l, 0:8, :] = u[l, 24:32, :]
            old_w, old_e = uw[l, 5:13, :], ue[l, 5:13, :]
        else:
            old_w, old_e = u[l, 5:13, :], u[l, 37:45, :]
        u_out[l, 5:13, :] = (old_w - difference(lambda k: pw[l, 5 + k : 13 + k, :])) * ok_w
        u_out[l, 37:45, :] = (old_e - difference(lambda k: pe[l, 5 + k : 13 + k, :])) * ok_e
        rhs_w = rest[l, 0:8, :] - difference(lambda k: u_out[l, 8 + k : 16 + k, :])
        rhs_e = rest[l, 8:16, :] - difference(lambda k: u_out[l, 32 + k : 40 + k, :])
        rhs = jnp.concatenate([rhs_w, rhs_e], axis=0)
        il = jnp.concatenate([inv[l, 0:8, :], inv[l, 24:32, :]], axis=0)
        gl = jnp.concatenate([g[l, 0:8, :], g[l, 24:32, :]], axis=0)
        w = rhs * il + gl * w
        w_buf[l] = w
    q = jnp.zeros((16, 128), F32)
    for l in range(63, -1, -1):
        gl = jnp.concatenate([g[l, 0:8, :], g[l, 24:32, :]], axis=0)
        q = w_buf[l] + gl * q
        p_out[l, 0:8, :] = q[0:8]
        p_out[l, 24:32, :] = q[8:16]
        w_buf[l] = q
    if first_step:
        write_edges((((w_buf.at[:, 0:8, :], 6),), ((w_buf.at[:, 8:16, :], 6),)), even, first, second)
    else:
        for l in range(64):
            east[6 * l : 6 * l + 3, :] = w_buf[l, 0:3, :]
            east[6 * l + 3 : 6 * l + 6, :] = v[l, 0:3, :]
        for b in range(8):
            east[384 + 8 * b : 392 + 8 * b, :] = pn[b, 0:8, :]


def north_pack_kernel(u, v, p, pe, out):
    lanes = lane_index()
    for b in range(8):
        strip = None
        for m in range(8):
            l = 8 * b + m
            for f, val in enumerate((u[l, 8:40, :], v[l], p[l])):
                at = 16 * m + 3 * f
                moved = roll_lanes(val, at)
                strip = moved if strip is None else jnp.where(lanes >= at, moved, strip)
        out[b, 0:32, :] = strip
        out[b, 32:40, :] = pe[b]


def turn_kernel(offsets, u, v, p, pe, ru, rv, rp, tail):
    shift = lax.rem(128 - offsets[1], 128)
    last_east = lax.axis_index("gx") == lax.axis_size("gx") - 1
    for l in range(64):
        ru[l] = pltpu.roll(u[l, 8:40, :], shift, 1)
        rv[l] = pltpu.roll(v[l], shift, 1)
        rp[l] = pltpu.roll(p[l], shift, 1)
        tail[0, l] = pltpu.roll(jnp.where(last_east, pe[0, l], u[l, 40:48, :]), shift, 1)
        tail[1, l] = pltpu.roll(pe[1, l], shift, 1)
        tail[2, l] = pltpu.roll(pe[2, l], shift, 1)


def move_kernel(offsets, ru, rv, rp, tail, e, north, ne, pn, ou, ov, op, bu, bv, bp, ext, ns, sems):
    lanes = lane_index()
    o0, o1 = offsets[0], offsets[1]
    last_east = lax.axis_index("gx") == lax.axis_size("gx") - 1
    last_north = lax.axis_index("gy") == lax.axis_size("gy") - 1
    own_lane = lanes < 128 - o1
    shift = lax.rem(128 - o1, 128)
    copies = []
    for b in range(8):
        ns[b, 0:32, :] = jnp.where(last_north, pn[b, 0:32, :], north[b, 0:32, :])
        top = jnp.where(last_east, pn[b, 32:40, :], e[384 + 8 * b : 392 + 8 * b, :])
        low = jnp.where(last_east, north[b, 32:40, :], ne[b])
        ns[b, 32:40, :] = jnp.where(last_north, top, low)
        nrow = ns[b, pl.ds(o0, 32), :]
        for m in range(8):
            l = 8 * b + m
            new = pltpu.roll(e[6 * l : 6 * l + 6, :], shift, 1)
            for f, (src, buf) in enumerate(((ru, bu), (rv, bv), (rp, bp))):
                ext[f, l, 0:8, :] = src[l, 24:32, :]
                ext[f, l, 8:16, :] = tail[f, l]
                if f > 0:
                    part = new[3:6] if f == 1 else new[0:3]
                    ext[f, l, 8:11, :] = jnp.where(last_east, tail[f, l, 0:3, :], part)
                back = lax.rem(256 - (16 * m + 3 * f) - o1, 128)
                strip = pltpu.roll(nrow, back, 1)
                buf[l, 0:24, :] = jnp.where(own_lane, src[l, pl.ds(o0, 24), :], strip[0:24])
                buf[l, 24:32, :] = jnp.where(own_lane, ext[f, l, pl.ds(o0, 8), :], strip[24:32])
        for f, (buf, out) in enumerate(((bu, ou), (bv, ov), (bp, op))):
            part = pl.ds(8 * b, 8)
            copy = pltpu.make_async_copy(buf.at[part], out.at[part], sems.at[8 * f + b])
            copy.start()
            copies.append(copy)
    for copy in copies:
        copy.wait()


VMEM = pl.BlockSpec(memory_space=pltpu.VMEM)
SMEM = pl.BlockSpec(memory_space=pltpu.SMEM)
ANY = pl.BlockSpec(memory_space=pl.ANY)


def sds(*shape):
    return jax.ShapeDtypeStruct(shape, F32)


def buffers(*shapes):
    return [pltpu.VMEM(shape, F32) for shape in shapes]


def call(body, out_shape, args, scratch=(), name=None, specs=None, outs=None, alias=None, us=1.0):
    specs = {} if specs is None else specs
    return pl.pallas_call(
        body,
        out_shape=out_shape,
        in_specs=[specs.get(k, VMEM) for k in range(len(args))],
        out_specs=jax.tree.map(lambda _: outs or VMEM, out_shape),
        scratch_shapes=list(scratch),
        input_output_aliases=alias or {},
        name=name,
        cost_estimate=pl.CostEstimate(flops=0, bytes_accessed=int(us * 3.2e6), transcendentals=0),
        compiler_params=pltpu.CompilerParams(vmem_limit_bytes=16 << 20),
    )(*args)


def on_device(wind_east, wind_north, pressure, stiffness, parent_east, parent_north, parent_corner, offsets):
    nx, ny = lax.axis_size("gx"), lax.axis_size("gy")
    mat = jnp.asarray(band(), BF16)
    x_in, x_out = swaps(nx)
    y_in, y_out = swaps(ny)
    field, padded, outer = sds(64, 32, 128), sds(64, 48, 128), sds(64, 16, 128)
    dma = pltpu.SemaphoreType.DMA

    first, second = call(
        x_edges_kernel,
        (sds(576, 128), sds(576, 128)),
        (pressure, wind_east),
        buffers(*[(64, 8, 128)] * 4) + [dma((4,))],
        name="x_edges",
        specs={0: ANY, 1: ANY},
    )
    x2 = lax.ppermute(second, "gx", x_out)
    x1 = lax.ppermute(first, "gx", x_in)
    strip = call(y_edges_kernel, sds(12, 32, 128), (pressure, wind_north), name="y_edges")
    y1 = lax.ppermute(strip, "gy", y_in)
    y2 = lax.ppermute(strip, "gy", y_out)
    inv, g = call(coefficients_kernel, (field, field), (stiffness,), name="coefficients")

    def strips(value):
        rows = value.shape[2]
        value = value.reshape(3, 8, 8, rows, 3).transpose(1, 3, 2, 0, 4).reshape(8, rows, 8, 9)
        return jnp.pad(value, ((0, 0), (0, 0), (0, 0), (0, 7))).reshape(8, rows, 128)

    pe_strip = jnp.pad(strips(parent_east[:, :, :, :3]), ((0, 0), (0, 5), (0, 0)))
    pn_strip = jnp.concatenate([strips(parent_north), strips(parent_corner)], axis=1)
    pn_strip = jnp.pad(pn_strip, ((0, 0), (0, 5), (0, 0)))
    pe_rows = jnp.pad(parent_east, ((0, 0), (0, 0), (0, 5), (0, 0)))

    p1, u1, v1, vh1, rest = call(
        functools.partial(inner_kernel, True),
        (field, padded, field, field, outer),
        (pressure, wind_east, wind_north, inv, g, mat, y1, y2, pe_strip, pn_strip, pe_rows),
        buffers((64, 16, 128)),
        name="inner1",
        specs={8: ANY, 9: ANY, 10: ANY},
        us=3.0,
    )
    p1, u1, first, second = call(
        functools.partial(outer_kernel, True),
        (field, padded, sds(384, 128), sds(384, 128)),
        (x1, x2, pressure, wind_east, inv, g, rest, p1, u1),
        buffers(*[(64, 16, 128)] * 5),
        name="outer1",
        alias={7: 0, 8: 1},
    )
    x2 = lax.ppermute(second, "gx", x_out)
    x1 = lax.ppermute(first, "gx", x_in)
    strip = call(y_pack_kernel, sds(8, 32, 128), (p1,), name="y_pack")
    y1 = lax.ppermute(strip, "gy", y_in)
    y2 = lax.ppermute(strip, "gy", y_out)
    p2, u2, v2, rest = call(
        functools.partial(inner_kernel, False),
        (field, padded, field, outer),
        (p1, u1, v1, vh1, inv, g, mat, y1, y2),
        buffers((64, 16, 128)),
        name="inner2",
        us=3.0,
    )
    p2, u2, east = call(
        functools.partial(outer_kernel, False),
        (field, padded, sds(448, 128)),
        (x1, x2, p1, u1, inv, g, rest, p2, u2, v2, pn_strip),
        buffers(*[(64, 16, 128)] * 3),
        name="outer2",
        alias={7: 0, 8: 1},
    )
    down_x = [(i, (i - 1) % nx) for i in range(nx)]
    down_y = [(j, (j - 1) % ny) for j in range(ny)]
    down = [(i * ny + j, (i - 1) % nx * ny + (j - 1) % ny) for i in range(nx) for j in range(ny)]
    from_east = lax.ppermute(east, "gx", down_x)
    north = call(north_pack_kernel, sds(8, 40, 128), (u2, v2, p2, pe_strip), name="north_pack")
    from_north = lax.ppermute(north, "gy", down_y)
    from_both = lax.ppermute(north[:, :8, :], ("gx", "gy"), down)
    ru, rv, rp, tail = call(
        turn_kernel,
        (field, field, field, sds(3, 64, 8, 128)),
        (offsets, u2, v2, p2, pe_rows),
        name="turn",
        specs={0: SMEM},
        us=1.0,
    )
    return call(
        move_kernel,
        (field, field, field),
        (offsets, ru, rv, rp, tail, from_east, from_north, from_both, pn_strip),
        buffers(*[(64, 32, 128)] * 3, (3, 64, 16, 128), (8, 40, 128)) + [dma((24,))],
        name="move",
        specs={0: SMEM},
        outs=ANY,
    )


def solution(mesh):
    in_specs = (
        P(None, "gx", "gy"),
        P(None, "gx", "gy"),
        P(None, "gx", "gy"),
        P("gx", "gy"),
        P(None, None, None, "gy"),
        P(None, None, "gx", None),
        P(),
        P(),
    )
    out_specs = (P(None, "gx", "gy"), P(None, "gx", "gy"), P(None, "gx", "gy"))
    return jax.shard_map(
        on_device, mesh=mesh, in_specs=in_specs, out_specs=out_specs, check_vma=False
    )
```

profile of v0, /device:TPU:31, one launch (start us, length us, event | category | flops | bytes accessed | tf_op | source)
XLA Modules:
  0.0 66.5 jit_solution(15993323557042366021)
XLA Ops:
  0.6 0.0 copy-start
  0.6 1.2 %copy-done = f32[64,32,128]{2,1,0:T(8,128)S(1)} copy-done((f32[64,32,128]{2,1,0:T(8,128)S(1)}, f32[64,32,128]{2,1,0:T(8,128)}, u32[]{:S(2)}) %copy-start) | copy-done | bytes 1048600
  1.9 0.0 copy-start.3
  1.9 1.2 %copy-done.3 = f32[64,32,128]{2,1,0:T(8,128)S(1)} copy-done((f32[64,32,128]{2,1,0:T(8,128)S(1)}, f32[64,32,128]{2,1,0:T(8,128)}, u32[]{:S(2)}) %copy-start.3) | copy-done | bytes 1048600
  3.1 0.0 copy-start.2
  3.1 1.3 %y_edges.1 = f32[12,32,128]{2,1,0:T(8,128)} custom-call(f32[64,32,128]{2,1,0:T(8,128)S(1)} %copy-done, f32[64,32,128]{2,1,0:T(8,128)S(1)} %copy-done.3), custom_call_target="tpu_custom_call" | custom-call | bytes 3200000 | tf_op jit(solution)/shard_map/y_edges/pallas_call | solution.py:328
  4.4 4.1 %collective-permute-start.3 = (f32[12,32,128]{2,1,0:T(8,128)}, f32[12,32,128]{2,1,0:T(8,128)S(1)}, u32[]{:S(2)}, u32[]{:S(2)}) collective-permute-start(f32[12,32,128]{2,1,0:T(8,128)} %y_edges.1), channel_id=1, source_target_pairs={{0,0},{1,2},{2,1},{3,4},{4,3},{5,6},{6,5},{7,8},{8,7},{9,10},{10,9... | collective-permute-start | bytes 589832 | tf_op jit(solution)/shard_map/ppermute | solution.py:361
  8.5 0.1 collective-permute-start.2
  8.6 0.0 copy-done.2
  8.6 1.1 %x_edges.1 = (f32[576,128]{1,0:T(8,128)}, f32[576,128]{1,0:T(8,128)}) custom-call(f32[64,32,128]{2,1,0:T(8,128)S(1)} %copy-done, f32[64,32,128]{2,1,0:T(8,128)S(1)} %copy-done.2), custom_call_target="tpu_custom_call" | custom-call | bytes 3200000 | tf_op jit(solution)/shard_map/x_edges/pallas_call | solution.py:328
  9.8 0.0 copy-start.9
  9.8 0.5 collective-permute-start
  10.3 5.7 %collective-permute-start.1 = (f32[576,128]{1,0:T(8,128)}, f32[576,128]{1,0:T(8,128)}, u32[]{:S(2)}, u32[]{:S(2)}) collective-permute-start(f32[576,128]{1,0:T(8,128)} %get-tuple-element.28), channel_id=1, source_target_pairs={{0,0},{16,32},{32,16},{48,64},{64,48},{80,96},{96,80},{112,112},{1... | collective-permute-start | bytes 884744 | tf_op jit(solution)/shard_map/ppermute | solution.py:357
  16.0 0.0 copy-done.8
  16.0 0.7 %slice_bitcast_fusion = f32[3,8,8,3,3]{4,2,1,3,0:T(8,128)} fusion(f32[3,64,3,128]{3,1,2,0:T(8,128)S(1)} %copy-done.8), kind=kLoop, calls=%fused_computation | loop fusion | bytes 13824 | tf_op jit(solution)/shard_map/reshape | solution.py:366
  16.8 0.9 %copy.30 = f32[3,64,3,128]{3,2,1,0:T(4,128)} copy(f32[3,64,3,128]{3,1,2,0:T(8,128)S(1)} %copy-done.8) | data formatting | bytes 589824 | tf_op args[4]
  17.7 0.0 copy-done.10
  17.7 0.1 reshape.39
  17.8 0.2 copy.37
  18.1 0.1 reshape.43
  18.2 0.0 copy-done.9
  18.2 0.2 copy.23
  18.3 0.2 copy.36
  18.5 0.8 %pad.25.clone = f32[8,32,8,16]{1,3,2,0:T(8,128)} pad(f32[8,32,8,9]{1,3,2,0:T(8,128)S(1)} %copy.36, f32[]{:T(128)} %constant.4.clone.1), padding=0_0x0_0x0_0x0_7 | pad | bytes 204804 | tf_op jit(solution)/shard_map/jit(_pad)/pad | solution.py:367
  19.4 2.0 %copy.28 = f32[8,32,128]{2,1,0:T(8,128)} copy(f32[8,32,128]{1,2,0:T(8,128)} %bitcast.21) | data formatting | bytes 262144 | tf_op jit(solution)/shard_map/reshape | solution.py:367
  21.4 2.1 %copy.20 = f32[3,8,8,3,3]{2,1,4,0,3:T(8,128)} copy(f32[3,8,8,3,3]{4,2,1,3,0:T(8,128)} %slice_bitcast_fusion) | data formatting | bytes 13824 | tf_op jit(solution)/shard_map/reshape | solution.py:366
  23.5 1.8 %copy.35 = f32[8,3,8,9]{3,2,1,0:T(8,128)} copy(f32[8,3,8,9]{2,0,3,1:T(8,128)} %bitcast.24) | data formatting | bytes 13824
  25.3 1.5 %pad.23.clone = f32[8,3,8,16]{3,2,1,0:T(8,128)} pad(f32[8,3,8,9]{3,2,1,0:T(8,128)} %copy.35, f32[]{:T(128)} %constant.4.clone.1), padding=0_0x0_0x0_0x0_7 | pad | bytes 19204 | tf_op jit(solution)/shard_map/jit(_pad)/pad | solution.py:367
  26.8 1.0 %reshape.42 = f32[8,3,128]{2,1,0:T(4,128)S(1)} reshape(f32[8,3,8,16]{3,2,1,0:T(8,128)} %pad.23.clone) | data formatting | bytes 24576 | tf_op jit(solution)/shard_map/reshape | solution.py:367
  27.8 1.1 %pad.28.rest_7_.pe = f32[3,64,8,128]{3,2,1,0:T(8,128)S(1)} pad(f32[3,64,3,128]{3,2,1,0:T(4,128)} %copy.30, f32[]{:T(128)} %constant.4.clone.1), padding=0_0x0_0x0_5x0_0 | pad | bytes 1081348 | tf_op jit(solution)/shard_map/jit(_pad)/pad | solution.py:372
  28.9 0.0 copy-done.6
  28.9 0.6 coefficients.1
  29.5 0.9 %select_maximum_fusion.rest_6_.tail_1_.pn = f32[8,40,128]{2,1,0:T(8,128)S(1)} fusion(f32[8,3,128]{2,1,0:T(4,128)S(1)} %reshape.43, f32[8,32,128]{2,1,0:T(8,128)} %copy.28), kind=kLoop, calls=%fused_computation.1 | loop fusion | flops 163840 | bytes 307200 | tf_op jit(solution)/shard_map/concatenate | solution.py:370
  30.4 0.0 collective-permute-done.3.rest_4_
  30.4 0.0 collective-permute-done.2.rest_3_
  30.4 0.0 copy-done.1
  30.4 0.0 copy-done.4
  30.4 0.0 copy-done.5
  30.4 3.0 %inner1.1 = (f32[64,32,128]{2,1,0:T(8,128)S(1)}, f32[64,48,128]{2,1,0:T(8,128)S(1)}, f32[64,32,128]{2,1,0:T(8,128)S(1)}, f32[64,32,128]{2,1,0:T(8,128)S(1)}, f32[64,16,128]{2,1,0:T(8,128)S(1)}) custom-call(f32[64,32,128]{2,1,0:T(8,128)S(1)} %copy-done.1, f32[64,32,128]{2,1,0:T(8,128)S(1)} %copy-done.2, f32[64,32,128]{2,1,0:T(8,128)S(1)} %copy-done.4, ...), custom_call_target="tpu_custom_call" | custom-call | bytes 9600000 | tf_op jit(solution)/shard_map/inner1/pallas_call | solution.py:328
  33.5 0.0 collective-permute-done.x1
  33.5 0.0 collective-permute-done.1.x2
  33.5 2.0 %outer1.1 = (f32[64,32,128]{2,1,0:T(8,128)S(1)}, f32[64,48,128]{2,1,0:T(8,128)S(1)}, f32[384,128]{1,0:T(8,128)S(1)}, f32[384,128]{1,0:T(8,128)S(1)}) custom-call(f32[576,128]{1,0:T(8,128)} %collective-permute-done.x1, f32[576,128]{1,0:T(8,128)} %collective-permute-done.1.x2, ...), custom_call_target="tpu_custom_call", output_to_operand_aliasing={{0}: (7, {}), {1}: (8, {})} | custom-call | bytes 3200000 | tf_op jit(solution)/shard_map/outer1/pallas_call | solution.py:328
  35.5 0.1 collective-permute-start.4
  35.6 4.2 %collective-permute-start.5 = (f32[384,128]{1,0:T(8,128)S(1)}, f32[384,128]{1,0:T(8,128)S(1)}, u32[]{:S(2)}, u32[]{:S(2)}) collective-permute-start(f32[384,128]{1,0:T(8,128)S(1)} %get-tuple-element.35), channel_id=1, source_target_pairs={{0,0},{16,32},{32,16},{48,64},{64,48},{80,96},{96,80},{112,112},{1... | collective-permute-start | bytes 589832 | tf_op jit(solution)/shard_map/ppermute | solution.py:391
  39.8 0.3 y_pack.1
  40.1 4.5 %collective-permute-start.7 = (f32[8,32,128]{2,1,0:T(8,128)S(1)}, f32[8,32,128]{2,1,0:T(8,128)S(1)}, u32[]{:S(2)}, u32[]{:S(2)}) collective-permute-start(f32[8,32,128]{2,1,0:T(8,128)S(1)} %y_pack.1), channel_id=1, source_target_pairs={{0,0},{1,2},{2,1},{3,4},{4,3},{5,6},{6,5},{7,8},{8,7},{9,10},{10,9... | collective-permute-start | bytes 393224 | tf_op jit(solution)/shard_map/ppermute | solution.py:395
  44.6 0.1 collective-permute-start.6
  44.7 3.9 %collective-permute-done.7.rest_5_ = f32[8,32,128]{2,1,0:T(8,128)S(1)} collective-permute-done((f32[8,32,128]{2,1,0:T(8,128)S(1)}, f32[8,32,128]{2,1,0:T(8,128)S(1)}, u32[]{:S(2)}, u32[]{:S(2)}) %collective-permute-start.7) | collective-permute-done | bytes 131104 | tf_op jit(solution)/shard_map/ppermute | solution.py:395
  48.6 0.0 collective-permute-done.6.rest_4_
  48.6 2.1 %inner2.1 = (f32[64,32,128]{2,1,0:T(8,128)S(1)}, f32[64,48,128]{2,1,0:T(8,128)S(1)}, f32[64,32,128]{2,1,0:T(8,128)S(1)}, f32[64,16,128]{2,1,0:T(8,128)S(1)}) custom-call(f32[64,32,128]{2,1,0:T(8,128)S(1)} %get-tuple-element.36.p, f32[64,48,128]{2,1,0:T(8,128)S(1)} %get-tuple-element.37.u, f32[64,32,128]{2,1,0:T(8,128)S(1)} %get-tuple-element.38.v, ...), custom_call_target="tpu_custom_call" | custom-call | bytes 9600000 | tf_op jit(solution)/shard_map/inner2/pallas_call | solution.py:328
  50.7 0.0 collective-permute-done.4.x1
  50.7 0.0 collective-permute-done.5.x2
  50.7 0.9 %outer2.1 = (f32[64,32,128]{2,1,0:T(8,128)S(1)}, f32[64,48,128]{2,1,0:T(8,128)S(1)}, f32[448,128]{1,0:T(8,128)S(1)}) custom-call(f32[384,128]{1,0:T(8,128)S(1)} %collective-permute-done.4.x1, f32[384,128]{1,0:T(8,128)S(1)} %collective-permute-done.5.x2, f32[64,32,128]{2,1,0:T(8,128)S(1)} %get-tuple-element.36.p, ...), custom_call_target="tpu_custom_call", output_to_operand_aliasing={{0}: (7, {}), {1}: (8, {})} | custom-call | bytes 3200000 | tf_op jit(solution)/shard_map/outer2/pallas_call | solution.py:328
  51.6 0.1 collective-permute-start.8
  51.7 0.0 copy-start.7
  51.7 0.8 %north_pack.1 = f32[8,40,128]{2,1,0:T(8,128)S(1)} custom-call(f32[64,48,128]{2,1,0:T(8,128)S(1)} %get-tuple-element.44.u, f32[64,32,128]{2,1,0:T(8,128)S(1)} %get-tuple-element.43.tail_0_.v, f32[64,32,128]{2,1,0:T(8,128)S(1)} %get-tuple-element.45.p, f32[8,8,128]{2,1,0:T(8,128)S(1)} %pad.24.rest_5_.pe), custom_call_target="tpu_custom_call" | custom-call | bytes 3200000 | tf_op jit(solution)/shard_map/north_pack/pallas_call | solution.py:328
  52.6 0.1 collective-permute-start.9
  52.7 0.2 collective-permute-start.10
  52.9 0.0 copy-done.7
  52.9 1.6 %turn.1 = (f32[64,32,128]{2,1,0:T(8,128)S(1)}, f32[64,32,128]{2,1,0:T(8,128)S(1)}, f32[64,32,128]{2,1,0:T(8,128)S(1)}, f32[3,64,8,128]{3,2,1,0:T(8,128)S(1)}) custom-call(s32[2]{0:T(128)S(1)} %copy-done.7, f32[64,48,128]{2,1,0:T(8,128)S(1)} %get-tuple-element.44.u, f32[64,32,128]{2,1,0:T(8,128)S(1)} %get-tuple-element.43.tail_0_.v, ...), custom_call_target="tpu_custom_call" | custom-call | bytes 3200000 | tf_op jit(solution)/shard_map/turn/pallas_call | solution.py:328
  54.5 9.2 %collective-permute-done.10.ne = f32[8,8,128]{2,1,0:T(8,128)S(1)} collective-permute-done((f32[8,8,128]{2,1,0:T(8,128)S(1)}, f32[8,8,128]{2,1,0:T(8,128)S(1)}, u32[]{:S(2)}, u32[]{:S(2)}) %collective-permute-start.10) | collective-permute-done | bytes 32800 | tf_op jit(solution)/shard_map/ppermute | solution.py:418
  63.7 0.0 collective-permute-done.9.north
  63.7 0.0 collective-permute-done.8.e
  63.7 2.8 %move.1 = (f32[64,32,128]{2,1,0:T(8,128)}, f32[64,32,128]{2,1,0:T(8,128)}, f32[64,32,128]{2,1,0:T(8,128)}) custom-call(s32[2]{0:T(128)S(1)} %copy-done.7, f32[64,32,128]{2,1,0:T(8,128)S(1)} %get-tuple-element.46.ru, f32[64,32,128]{2,1,0:T(8,128)S(1)} %get-tuple-element.47.rv, f32[64,32,128]{2,1,0:T(8,128)S(1)} %get-tuple-element.48.rp, ...), custom_call_target="tpu_custom_call" | custom-call | bytes 3200000 | tf_op jit(solution)/shard_map/move/pallas_call | solution.py:328
  (10 shorter events, 0.0 us)
Async XLA Ops:
  0.6 1.2 %copy-start = (f32[64,32,128]{2,1,0:T(8,128)S(1)}, f32[64,32,128]{2,1,0:T(8,128)}, u32[]{:S(2)}) copy-start(f32[64,32,128]{2,1,0:T(8,128)} %p.7) | copy-start | bytes 3145732
  1.9 1.2 %copy-start.3 = (f32[64,32,128]{2,1,0:T(8,128)S(1)}, f32[64,32,128]{2,1,0:T(8,128)}, u32[]{:S(2)}) copy-start(f32[64,32,128]{2,1,0:T(8,128)} %v.3) | copy-start | bytes 3145732
  3.1 5.5 %copy-start.2 = (f32[64,32,128]{2,1,0:T(8,128)S(1)}, f32[64,32,128]{2,1,0:T(8,128)}, u32[]{:S(2)}) copy-start(f32[64,32,128]{2,1,0:T(8,128)} %u.5) | copy-start | bytes 3145732
  4.4 11.6 %copy-start.8 = (f32[3,64,3,128]{3,1,2,0:T(8,128)S(1)}, f32[3,64,3,128]{3,1,2,0:T(8,128)}, u32[]{:S(2)}) copy-start(f32[3,64,3,128]{3,1,2,0:T(8,128)} %param.13) | copy-start | bytes 884740
  4.4 13.3 %copy-start.10 = (f32[3,64,3,3]{1,3,2,0:T(4,128)S(1)}, f32[3,64,3,3]{1,3,2,0:T(4,128)}, u32[]{:S(2)}) copy-start(f32[3,64,3,3]{1,3,2,0:T(4,128)} %param.15) | copy-start | bytes 20740
  4.4 26.0 %collective-permute-start.3 = (f32[12,32,128]{2,1,0:T(8,128)}, f32[12,32,128]{2,1,0:T(8,128)S(1)}, u32[]{:S(2)}, u32[]{:S(2)}) collective-permute-start(f32[12,32,128]{2,1,0:T(8,128)} %y_edges.1), channel_id=1, source_target_pairs={{0,0},{1,2},{2,1},{3,4},{4,3},{5,6},{6,5},{7,8},{8,7},{9,10},{10,9... | collective-permute-start | bytes 589832 | tf_op jit(solution)/shard_map/ppermute | solution.py:361
  8.5 21.9 %collective-permute-start.2 = (f32[12,32,128]{2,1,0:T(8,128)}, f32[12,32,128]{2,1,0:T(8,128)}, u32[]{:S(2)}, u32[]{:S(2)}) collective-permute-start(f32[12,32,128]{2,1,0:T(8,128)} %y_edges.1), channel_id=1, source_target_pairs={{0,1},{1,0},{2,3},{3,2},{4,5},{5,4},{6,7},{7,6},{8,9},{9,8},{10,11... | collective-permute-start | bytes 589832 | tf_op jit(solution)/shard_map/ppermute | solution.py:360
  9.8 8.4 %copy-start.9 = (f32[3,64,32,3]{1,2,3,0:T(8,128)S(1)}, f32[3,64,32,3]{1,2,3,0:T(8,128)}, u32[]{:S(2)}) copy-start(f32[3,64,32,3]{1,2,3,0:T(8,128)} %param.14) | copy-start | bytes 221188
  9.8 23.7 %collective-permute-start = (f32[576,128]{1,0:T(8,128)}, f32[576,128]{1,0:T(8,128)}, u32[]{:S(2)}, u32[]{:S(2)}) collective-permute-start(f32[576,128]{1,0:T(8,128)} %get-tuple-element.27), channel_id=1, source_target_pairs={{0,16},{16,0},{32,48},{48,32},{64,80},{80,64},{96,112},{112,96},{1... | collective-permute-start | bytes 884744 | tf_op jit(solution)/shard_map/ppermute | solution.py:358
  10.3 23.2 %collective-permute-start.1 = (f32[576,128]{1,0:T(8,128)}, f32[576,128]{1,0:T(8,128)}, u32[]{:S(2)}, u32[]{:S(2)}) collective-permute-start(f32[576,128]{1,0:T(8,128)} %get-tuple-element.28), channel_id=1, source_target_pairs={{0,0},{16,32},{32,16},{48,64},{64,48},{80,96},{96,80},{112,112},{1... | collective-permute-start | bytes 884744 | tf_op jit(solution)/shard_map/ppermute | solution.py:357
  19.4 9.5 %copy-start.6 = (f32[32,128]{1,0:T(8,128)S(1)}, f32[32,128]{1,0:T(8,128)}, u32[]{:S(2)}) copy-start(f32[32,128]{1,0:T(8,128)} %s_ref.1) | copy-start | bytes 49156
  19.4 11.0 %copy-start.1 = (f32[64,32,128]{2,1,0:T(8,128)S(1)}, f32[64,32,128]{2,1,0:T(8,128)}, u32[]{:S(2)}) copy-start(f32[64,32,128]{2,1,0:T(8,128)} %p.7) | copy-start | bytes 3145732
  19.4 11.0 %copy-start.4 = (f32[64,32,128]{2,1,0:T(8,128)S(1)}, f32[64,32,128]{2,1,0:T(8,128)}, u32[]{:S(2)}) copy-start(f32[64,32,128]{2,1,0:T(8,128)} %v.3) | copy-start | bytes 3145732
  19.4 11.0 %copy-start.5 = (bf16[256,256]{1,0:T(8,128)(2,1)S(1)}, bf16[256,256]{1,0:T(8,128)(2,1)}, u32[]{:S(2)}) copy-start(bf16[256,256]{1,0:T(8,128)(2,1)} %constant.5.clone.rest_2_.rest_3_) | copy-start | bytes 393220
  35.5 15.2 %collective-permute-start.4 = (f32[384,128]{1,0:T(8,128)S(1)}, f32[384,128]{1,0:T(8,128)S(1)}, u32[]{:S(2)}, u32[]{:S(2)}) collective-permute-start(f32[384,128]{1,0:T(8,128)S(1)} %get-tuple-element.34), channel_id=1, source_target_pairs={{0,16},{16,0},{32,48},{48,32},{64,80},{80,64},{96,112},{112,96},{1... | collective-permute-start | bytes 589832 | tf_op jit(solution)/shard_map/ppermute | solution.py:392
  35.6 15.1 %collective-permute-start.5 = (f32[384,128]{1,0:T(8,128)S(1)}, f32[384,128]{1,0:T(8,128)S(1)}, u32[]{:S(2)}, u32[]{:S(2)}) collective-permute-start(f32[384,128]{1,0:T(8,128)S(1)} %get-tuple-element.35), channel_id=1, source_target_pairs={{0,0},{16,32},{32,16},{48,64},{64,48},{80,96},{96,80},{112,112},{1... | collective-permute-start | bytes 589832 | tf_op jit(solution)/shard_map/ppermute | solution.py:391
  40.1 8.5 %collective-permute-start.7 = (f32[8,32,128]{2,1,0:T(8,128)S(1)}, f32[8,32,128]{2,1,0:T(8,128)S(1)}, u32[]{:S(2)}, u32[]{:S(2)}) collective-permute-start(f32[8,32,128]{2,1,0:T(8,128)S(1)} %y_pack.1), channel_id=1, source_target_pairs={{0,0},{1,2},{2,1},{3,4},{4,3},{5,6},{6,5},{7,8},{8,7},{9,10},{10,9... | collective-permute-start | bytes 393224 | tf_op jit(solution)/shard_map/ppermute | solution.py:395
  44.6 4.0 %collective-permute-start.6 = (f32[8,32,128]{2,1,0:T(8,128)S(1)}, f32[8,32,128]{2,1,0:T(8,128)S(1)}, u32[]{:S(2)}, u32[]{:S(2)}) collective-permute-start(f32[8,32,128]{2,1,0:T(8,128)S(1)} %y_pack.1), channel_id=1, source_target_pairs={{0,1},{1,0},{2,3},{3,2},{4,5},{5,4},{6,7},{7,6},{8,9},{9,8},{10,11... | collective-permute-start | bytes 393224 | tf_op jit(solution)/shard_map/ppermute | solution.py:394
  51.6 12.1 %collective-permute-start.8 = (f32[448,128]{1,0:T(8,128)S(1)}, f32[448,128]{1,0:T(8,128)S(1)}, u32[]{:S(2)}, u32[]{:S(2)}) collective-permute-start(f32[448,128]{1,0:T(8,128)S(1)} %get-tuple-element.50), channel_id=1, source_target_pairs={{0,112},{16,0},{32,16},{48,32},{64,48},{80,64},{96,80},{112,96},{1... | collective-permute-start | bytes 688136 | tf_op jit(solution)/shard_map/ppermute | solution.py:415
  51.7 1.2 %copy-start.7 = (s32[2]{0:T(128)S(1)}, s32[2]{0:T(128)}, u32[]{:S(2)}) copy-start(s32[2]{0:T(128)} %offsets.3) | copy-start | bytes 28
  52.6 11.1 %collective-permute-start.9 = (f32[8,40,128]{2,1,0:T(8,128)S(1)}, f32[8,40,128]{2,1,0:T(8,128)S(1)}, u32[]{:S(2)}, u32[]{:S(2)}) collective-permute-start(f32[8,40,128]{2,1,0:T(8,128)S(1)} %north_pack.1), channel_id=1, source_target_pairs={{0,15},{1,0},{2,1},{3,2},{4,3},{5,4},{6,5},{7,6},{8,7},{9,8},{10,9... | collective-permute-start | bytes 491528 | tf_op jit(solution)/shard_map/ppermute | solution.py:417
  52.7 11.1 %collective-permute-start.10 = (f32[8,8,128]{2,1,0:T(8,128)S(1)}, f32[8,8,128]{2,1,0:T(8,128)S(1)}, u32[]{:S(2)}, u32[]{:S(2)}) collective-permute-start(f32[8,8,128]{2,1,0:T(8,128)S(1)} %slice.8), channel_id=1, source_target_pairs={{0,127},{1,112},{2,113},{3,114},{4,115},{5,116},{6,117},{7,118},{8... | collective-permute-start | bytes 98312 | tf_op jit(solution)/shard_map/ppermute | solution.py:418
where the time goes:
time: 67.2 us; the launch traced here: 66.5 us
  starting transfers between devices  19.7 us (29%)
  Pallas kernels  16.5 us (25%)
  local copies, waits for them, and re-layouts  15.3 us (23%)
  waiting for transfers between devices  13.2 us (20%)
  between operations  0.95 us (1%)
  other arithmetic  0.92 us (1%)
    pallas_call x11, Pallas kernels, call(): pl.pallas_call(body, out_shape=out_shape, in_specs=[specs.get(k, VMEM) fo...  16.5 us
    ppermute x2, starting transfers between devices, on_device(): x2 = lax.ppermute(second, 'gx', x_out)  9.88 us
    ppermute x1, waiting for transfers between devices, on_device(): from_both = lax.ppermute(north[:, :8, :], ('gx', 'gy'), down)  9.2 us
    ppermute x2, starting transfers between devices, on_device(): y2 = lax.ppermute(strip, 'gy', y_out)  8.6 us
    unnamed x27, local copies, waits for them, and re-layouts  5.74 us
    ppermute x2, waiting for transfers between devices, on_device(): y2 = lax.ppermute(strip, 'gy', y_out)  3.94 us
    reshape x3, local copies, waits for them, and re-layouts, strips(): jnp.pad(value, ((0, 0), (0, 0), (0, 0), (0, 7))).reshape(8, rows, 128)  3.11 us
    reshape x4, local copies, waits for them, and re-layouts, strips(): value.reshape(3, 8, 8, rows, 3).transpose(1, 3, 2, 0, 4)  2.95 us
  transfers between devices with their start and end apart: 11, of which 2 were waited for; matrix products, arithmetic and copies ran while one was open for 21% of the time, Pallas kernels for 14%

commit v1 on v0

--- a/solution.py
+++ b/solution.py
@@ -86,7 +86,7 @@
     write_edges((((pw, 6), (uw, 3)), ((pe, 6), (ue, 3))), even, first, second)
 
 
-def y_edges_kernel(p, v, out):
+def y_edges_kernel(p, v, after, out):
     lanes = lane_index()
     for b in range(8):
         out[b] = pack([p[8 * b + m] for m in range(8)], 6, 16, lanes)
@@ -118,6 +118,16 @@
 
 def difference(at):
     return C1 * (at(1) - at(-1)) - C2 * (at(2) - at(-2)) + C3 * (at(3) - at(-3))
+
+
+def east_columns(out, field, pe, f):
+    for l in range(64):
+        out[3 * l : 3 * l + 3, :] = field[l, 0:3, :]
+
+    @pl.when(lax.axis_index("gx") == 0)
+    def _():
+        for x in range(3):
+            out[pl.ds(x, 64, stride=3), :] = pe[f, x]
 
 
 def inner_kernel(first_step, p, u, v, *rest):
@@ -179,7 +189,7 @@
     if first_step:
         p_out, u_out, first, second, pw, pe, uw, ue, w_buf = tail
     else:
-        v, pn, p_out, u_out, east, pw, pe, w_buf = tail
+        v, parent, p_out, u_out, east, pw, pe, w_buf = tail
     gx = lax.axis_index("gx")
     even = gx % 2 == 0
     in_w = gx > 0
@@ -241,15 +251,40 @@
     if first_step:
         write_edges((((w_buf.at[:, 0:8, :], 6),), ((w_buf.at[:, 8:16, :], 6),)), even, first, second)
     else:
-        for l in range(64):
-            east[6 * l : 6 * l + 3, :] = w_buf[l, 0:3, :]
-            east[6 * l + 3 : 6 * l + 6, :] = v[l, 0:3, :]
-        for b in range(8):
-            east[384 + 8 * b : 392 + 8 * b, :] = pn[b, 0:8, :]
-
-
-def north_pack_kernel(u, v, p, pe, out):
-    lanes = lane_index()
+        east_columns(east.at[0:192], v, parent, 1)
+        east_columns(east.at[192:384], w_buf, parent, 2)
+
+
+def parents_kernel(pe, pn, pc, pe_strip, pn_strip, rows, cells):
+    lanes = lane_index()
+    for f in range(3):
+        for x in range(3):
+            rows[pl.ds(512 * f + x, 64, stride=8), :] = pe[f, x]
+        for t in range(3):
+            cells[3 * f + t, 0:32, 0:64] = pn[f, t]
+            for x in range(3):
+                cells[3 * f + t, 32 + x : 33 + x, 0:64] = pc[f, x, t : t + 1, :]
+    lane = lax.broadcasted_iota(jnp.int32, (40, 128), 1)
+    for b in range(8):
+        strip = None
+        for m in range(8):
+            for f in range(3):
+                at = 16 * m + 3 * f
+                row = 512 * f + 8 * (8 * b + m)
+                moved = roll_lanes(rows[row : row + 8, :], at)
+                strip = moved if strip is None else jnp.where(lanes >= at, moved, strip)
+        pe_strip[b] = strip
+        strip = None
+        for r in range(9):
+            moved = jnp.take_along_axis(cells[r], 8 * b + lane // 16, axis=1, mode="promise_in_bounds")
+            strip = moved if strip is None else jnp.where(lane % 16 >= r, moved, strip)
+        pn_strip[b] = strip
+
+
+def north_pack_kernel(u, v, p, pe, pn, out, out_corner):
+    lanes = lane_index()
+    west = lax.axis_index("gx") == 0
+    south = lax.axis_index("gy") == 0
     for b in range(8):
         strip = None
         for m in range(8):
@@ -258,45 +293,45 @@
                 at = 16 * m + 3 * f
                 moved = roll_lanes(val, at)
                 strip = moved if strip is None else jnp.where(lanes >= at, moved, strip)
-        out[b, 0:32, :] = strip
-        out[b, 32:40, :] = pe[b]
+        out[b] = jnp.where(south, pn[b, 0:32, :], strip)
+        edge = jnp.where(west, pn[b, 32:40, :], pn[b, 0:8, :])
+        out_corner[b] = jnp.where(south, edge, jnp.where(west, pe[b], strip[0:8]))
 
 
 def turn_kernel(offsets, u, v, p, pe, ru, rv, rp, tail):
     shift = lax.rem(128 - offsets[1], 128)
-    last_east = lax.axis_index("gx") == lax.axis_size("gx") - 1
     for l in range(64):
         ru[l] = pltpu.roll(u[l, 8:40, :], shift, 1)
         rv[l] = pltpu.roll(v[l], shift, 1)
         rp[l] = pltpu.roll(p[l], shift, 1)
-        tail[0, l] = pltpu.roll(jnp.where(last_east, pe[0, l], u[l, 40:48, :]), shift, 1)
-        tail[1, l] = pltpu.roll(pe[1, l], shift, 1)
-        tail[2, l] = pltpu.roll(pe[2, l], shift, 1)
-
-
-def move_kernel(offsets, ru, rv, rp, tail, e, north, ne, pn, ou, ov, op, bu, bv, bp, ext, ns, sems):
+        tail[8 * l : 8 * l + 8, :] = pltpu.roll(u[l, 40:48, :], shift, 1)
+
+    @pl.when(lax.axis_index("gx") == lax.axis_size("gx") - 1)
+    def _():
+        for x in range(3):
+            tail[pl.ds(x, 64, stride=8), :] = pltpu.roll(pe[0, x], shift, 1)
+
+
+def move_kernel(offsets, ru, rv, rp, tail, east, north, corner, ou, ov, op, bu, bv, bp, ext, ns, columns, sems):
     lanes = lane_index()
     o0, o1 = offsets[0], offsets[1]
-    last_east = lax.axis_index("gx") == lax.axis_size("gx") - 1
-    last_north = lax.axis_index("gy") == lax.axis_size("gy") - 1
     own_lane = lanes < 128 - o1
     shift = lax.rem(128 - o1, 128)
+    columns[...] = pltpu.roll(east[...], shift, 1)
     copies = []
     for b in range(8):
-        ns[b, 0:32, :] = jnp.where(last_north, pn[b, 0:32, :], north[b, 0:32, :])
-        top = jnp.where(last_east, pn[b, 32:40, :], e[384 + 8 * b : 392 + 8 * b, :])
-        low = jnp.where(last_east, north[b, 32:40, :], ne[b])
-        ns[b, 32:40, :] = jnp.where(last_north, top, low)
+        ns[b, 0:32, :] = north[b]
+        ns[b, 32:40, :] = corner[b]
         nrow = ns[b, pl.ds(o0, 32), :]
         for m in range(8):
             l = 8 * b + m
-            new = pltpu.roll(e[6 * l : 6 * l + 6, :], shift, 1)
             for f, (src, buf) in enumerate(((ru, bu), (rv, bv), (rp, bp))):
                 ext[f, l, 0:8, :] = src[l, 24:32, :]
-                ext[f, l, 8:16, :] = tail[f, l]
-                if f > 0:
-                    part = new[3:6] if f == 1 else new[0:3]
-                    ext[f, l, 8:11, :] = jnp.where(last_east, tail[f, l, 0:3, :], part)
+                if f == 0:
+                    ext[f, l, 8:16, :] = tail[8 * l : 8 * l + 8, :]
+                else:
+                    at = 192 * (f - 1) + 3 * l
+                    ext[f, l, 8:11, :] = columns[at : at + 3, :]
                 back = lax.rem(256 - (16 * m + 3 * f) - o1, 128)
                 strip = pltpu.roll(nrow, back, 1)
                 buf[l, 0:24, :] = jnp.where(own_lane, src[l, pl.ds(o0, 24), :], strip[0:24])
@@ -313,6 +348,7 @@
 VMEM = pl.BlockSpec(memory_space=pltpu.VMEM)
 SMEM = pl.BlockSpec(memory_space=pltpu.SMEM)
 ANY = pl.BlockSpec(memory_space=pl.ANY)
+HBM = pl.BlockSpec(memory_space=pltpu.HBM)
 
 
 def sds(*shape):
@@ -323,7 +359,7 @@
     return [pltpu.VMEM(shape, F32) for shape in shapes]
 
 
-def call(body, out_shape, args, scratch=(), name=None, specs=None, outs=None, alias=None, us=1.0):
+def call(body, out_shape, args, scratch=(), name=None, specs=None, outs=None, alias=None, us=0.05, vmem=16):
     specs = {} if specs is None else specs
     return pl.pallas_call(
         body,
@@ -334,7 +370,7 @@
         input_output_aliases=alias or {},
         name=name,
         cost_estimate=pl.CostEstimate(flops=0, bytes_accessed=int(us * 3.2e6), transcendentals=0),
-        compiler_params=pltpu.CompilerParams(vmem_limit_bytes=16 << 20),
+        compiler_params=pltpu.CompilerParams(vmem_limit_bytes=vmem << 20),
     )(*args)
 
 
@@ -352,33 +388,33 @@
         (pressure, wind_east),
         buffers(*[(64, 8, 128)] * 4) + [dma((4,))],
         name="x_edges",
-        specs={0: ANY, 1: ANY},
+        specs={0: HBM, 1: HBM},
+        vmem=60,
     )
     x2 = lax.ppermute(second, "gx", x_out)
     x1 = lax.ppermute(first, "gx", x_in)
-    strip = call(y_edges_kernel, sds(12, 32, 128), (pressure, wind_north), name="y_edges")
+    strip = call(y_edges_kernel, sds(12, 32, 128), (pressure, wind_north, first), name="y_edges", specs={2: ANY})
     y1 = lax.ppermute(strip, "gy", y_in)
     y2 = lax.ppermute(strip, "gy", y_out)
     inv, g = call(coefficients_kernel, (field, field), (stiffness,), name="coefficients")
 
-    def strips(value):
-        rows = value.shape[2]
-        value = value.reshape(3, 8, 8, rows, 3).transpose(1, 3, 2, 0, 4).reshape(8, rows, 8, 9)
-        return jnp.pad(value, ((0, 0), (0, 0), (0, 0), (0, 7))).reshape(8, rows, 128)
-
-    pe_strip = jnp.pad(strips(parent_east[:, :, :, :3]), ((0, 0), (0, 5), (0, 0)))
-    pn_strip = jnp.concatenate([strips(parent_north), strips(parent_corner)], axis=1)
-    pn_strip = jnp.pad(pn_strip, ((0, 0), (0, 5), (0, 0)))
-    pe_rows = jnp.pad(parent_east, ((0, 0), (0, 0), (0, 5), (0, 0)))
+    pe = parent_east.transpose(0, 2, 1, 3)
+    pe_strip, pn_strip = call(
+        parents_kernel,
+        (sds(8, 8, 128), sds(8, 40, 128)),
+        (pe, parent_north.transpose(0, 3, 2, 1), parent_corner.transpose(0, 2, 3, 1)),
+        buffers((3 * 64 * 8, 128), (9, 40, 128)),
+        name="parents",
+    )
 
     p1, u1, v1, vh1, rest = call(
         functools.partial(inner_kernel, True),
         (field, padded, field, field, outer),
-        (pressure, wind_east, wind_north, inv, g, mat, y1, y2, pe_strip, pn_strip, pe_rows),
+        (pressure, wind_east, wind_north, inv, g, mat, y1, y2, pe_strip, pn_strip, pe),
         buffers((64, 16, 128)),
         name="inner1",
         specs={8: ANY, 9: ANY, 10: ANY},
-        us=3.0,
+        us=0.3,
     )
     p1, u1, first, second = call(
         functools.partial(outer_kernel, True),
@@ -399,36 +435,41 @@
         (p1, u1, v1, vh1, inv, g, mat, y1, y2),
         buffers((64, 16, 128)),
         name="inner2",
-        us=3.0,
-    )
+        us=0.3,
+    )
+    down_x = [(i, (i - 1) % nx) for i in range(nx)]
+    down_y = [(j, (j - 1) % ny) for j in range(ny)]
+    down = [(i * ny + j, (i - 1) % nx * ny + (j - 1) % ny) for i in range(nx) for j in range(ny)]
     p2, u2, east = call(
         functools.partial(outer_kernel, False),
-        (field, padded, sds(448, 128)),
-        (x1, x2, p1, u1, inv, g, rest, p2, u2, v2, pn_strip),
+        (field, padded, sds(384, 128)),
+        (x1, x2, p1, u1, inv, g, rest, p2, u2, v2, pe),
         buffers(*[(64, 16, 128)] * 3),
         name="outer2",
         alias={7: 0, 8: 1},
     )
-    down_x = [(i, (i - 1) % nx) for i in range(nx)]
-    down_y = [(j, (j - 1) % ny) for j in range(ny)]
-    down = [(i * ny + j, (i - 1) % nx * ny + (j - 1) % ny) for i in range(nx) for j in range(ny)]
-    from_east = lax.ppermute(east, "gx", down_x)
-    north = call(north_pack_kernel, sds(8, 40, 128), (u2, v2, p2, pe_strip), name="north_pack")
-    from_north = lax.ppermute(north, "gy", down_y)
-    from_both = lax.ppermute(north[:, :8, :], ("gx", "gy"), down)
+    east = lax.ppermute(east, "gx", down_x)
+    north, corner = call(
+        north_pack_kernel,
+        (sds(8, 32, 128), sds(8, 8, 128)),
+        (u2, v2, p2, pe_strip, pn_strip),
+        name="north_pack",
+    )
+    north = lax.ppermute(north, "gy", down_y)
+    corner = lax.ppermute(corner, ("gx", "gy"), down)
     ru, rv, rp, tail = call(
         turn_kernel,
-        (field, field, field, sds(3, 64, 8, 128)),
-        (offsets, u2, v2, p2, pe_rows),
+        (field, field, field, sds(512, 128)),
+        (offsets, u2, v2, p2, pe),
         name="turn",
         specs={0: SMEM},
-        us=1.0,
     )
     return call(
         move_kernel,
         (field, field, field),
-        (offsets, ru, rv, rp, tail, from_east, from_north, from_both, pn_strip),
-        buffers(*[(64, 32, 128)] * 3, (3, 64, 16, 128), (8, 40, 128)) + [dma((24,))],
+        (offsets, ru, rv, rp, tail, east, north, corner),
+        buffers(*[(64, 32, 128)] * 3, (3, 64, 16, 128), (8, 40, 128), (384, 128))
+        + [dma((24,))],
         name="move",
         specs={0: SMEM},
         outs=ANY,

time: 67.2 us -> 55.6 us (0.83)
  local copies, waits for them, and re-layouts: 15.3 us -> 1.01 us
  waiting for transfers between devices: 13.2 us -> 18.3 us
  other arithmetic: 0.92 us -> 0 us
  Pallas kernels: 16.5 us -> 15.7 us
    reshape x7 -> x0, local copies, waits for them, and re-layouts: 6.07 us -> none  [the longest x3 3.11 us: strips(): jnp.pad(value, ((0, 0), (0, 0), (0, 0), (0, 7))).reshape(8, rows, 128)]
    unnamed x27 -> x20, local copies, waits for them, and re-layouts: 5.74 us -> 1.01 us
    ppermute x2, waiting for transfers between devices: 3.94 us -> 8.49 us  [on_device(): y2 = lax.ppermute(strip, 'gy', y_out)]
    pad x5 -> x0, local copies, waits for them, and re-layouts: 3.46 us -> none  [the longest x3 2.4 us: strips(): jnp.pad(value, ((0, 0), (0, 0), (0, 0), (0, 7))).reshape(8, rows, 128)]
    ppermute x2, starting transfers between devices: 0.63 us -> 1.62 us  [on_device(): x1 = lax.ppermute(first, 'gx', x_in)]
    concatenate x1 -> x0, other arithmetic: 0.92 us -> none  [on_device(): jnp.concatenate([strips(parent_north), strips(parent_corner)], axis=1)]
    pallas_call x11 -> x12, Pallas kernels: 16.5 us -> 15.7 us  [call(): pl.pallas_call(body, out_shape=out_shape, in_specs=[specs.get(k, VMEM) fo...]
    ppermute x2, starting transfers between devices: 9.88 us -> 9.02 us  [on_device(): x2 = lax.ppermute(second, 'gx', x_out)]
  transfers between devices with their start and end apart: 11 -> 11, of which waited for: 2 -> 3; matrix products, arithmetic and copies ran while one was open for 21% -> 0% of each run, Pallas kernels for 14% -> 16%
where the time goes in v1:
time: 55.6 us; the launch traced here: 55.4 us
  starting transfers between devices  19.6 us (35%)
  waiting for transfers between devices  18.3 us (33%)
  Pallas kernels  15.7 us (28%)
  local copies, waits for them, and re-layouts  1.01 us (2%)
  between operations  0.92 us (2%)
    pallas_call x12, Pallas kernels, call(): pl.pallas_call(body, out_shape=out_shape, in_specs=[specs.get(k, VMEM) fo...  15.7 us
    ppermute x1, waiting for transfers between devices, on_device(): corner = lax.ppermute(corner, ('gx', 'gy'), down)  9.74 us
    ppermute x2, starting transfers between devices, on_device(): x2 = lax.ppermute(second, 'gx', x_out)  9.02 us
    ppermute x2, starting transfers between devices, on_device(): y2 = lax.ppermute(strip, 'gy', y_out)  8.54 us
    ppermute x2, waiting for transfers between devices, on_device(): y2 = lax.ppermute(strip, 'gy', y_out)  8.49 us
    ppermute x2, starting transfers between devices, on_device(): x1 = lax.ppermute(first, 'gx', x_in)  1.62 us
  transfers between devices with their start and end apart: 11, of which 3 were waited for; matrix products, arithmetic and copies ran while one was open for 0% of the time, Pallas kernels for 16%

profile of v1, /device:TPU:31, one launch (start us, length us, event | category | flops | bytes accessed | tf_op | source)
XLA Modules:
  0.0 55.4 jit_solution(5889096987339525047)
XLA Ops:
  0.6 0.0 copy-start
  0.6 0.0 copy-start.3
  0.7 2.3 %x_edges.1 = (f32[576,128]{1,0:T(8,128)}, f32[576,128]{1,0:T(8,128)}) custom-call(f32[64,32,128]{2,1,0:T(8,128)} %p.7, f32[64,32,128]{2,1,0:T(8,128)} %u.5), custom_call_target="tpu_custom_call" | custom-call | bytes 160000 | tf_op jit(solution)/shard_map/x_edges/pallas_call | solution.py:364
  2.9 0.0 copy-start.2
  3.0 0.0 copy-start.1
  3.0 0.0 copy-start.4
  3.0 5.3 %collective-permute-start.1 = (f32[576,128]{1,0:T(8,128)}, f32[576,128]{1,0:T(8,128)S(1)}, u32[]{:S(2)}, u32[]{:S(2)}) collective-permute-start(f32[576,128]{1,0:T(8,128)} %get-tuple-element.32), channel_id=1, source_target_pairs={{0,0},{16,32},{32,16},{48,64},{64,48},{80,96},{96,80},{112,112},{1... | collective-permute-start | bytes 884744 | tf_op jit(solution)/shard_map/ppermute | solution.py:394
  8.3 0.1 collective-permute-start
  8.4 0.0 copy-done
  8.4 0.0 copy-done.3
  8.4 0.0 copy-start.5
  8.4 1.0 %copy-done.5 = f32[576,128]{1,0:T(8,128)S(1)} copy-done((f32[576,128]{1,0:T(8,128)S(1)}, f32[576,128]{1,0:T(8,128)}, u32[]{:S(2)}) %copy-start.5) | copy-done | bytes 294936
  9.4 0.0 copy-start.8
  9.4 0.0 copy-start.6
  9.4 0.0 copy-start.7
  9.4 0.6 %y_edges.1 = f32[12,32,128]{2,1,0:T(8,128)S(1)} custom-call(f32[64,32,128]{2,1,0:T(8,128)S(1)} %copy-done, f32[64,32,128]{2,1,0:T(8,128)S(1)} %copy-done.3, f32[576,128]{1,0:T(8,128)S(1)} %copy-done.5), custom_call_target="tpu_custom_call" | custom-call | bytes 160000 | tf_op jit(solution)/shard_map/y_edges/pallas_call | solution.py:364
  10.0 3.4 %collective-permute-start.3 = (f32[12,32,128]{2,1,0:T(8,128)S(1)}, f32[12,32,128]{2,1,0:T(8,128)S(1)}, u32[]{:S(2)}, u32[]{:S(2)}) collective-permute-start(f32[12,32,128]{2,1,0:T(8,128)S(1)} %y_edges.1), channel_id=1, source_target_pairs={{0,0},{1,2},{2,1},{3,4},{4,3},{5,6},{6,5},{7,8},{8,7},{9,10},{10,9... | collective-permute-start | bytes 589832 | tf_op jit(solution)/shard_map/ppermute | solution.py:398
  13.4 0.1 collective-permute-start.2
  13.5 0.0 copy-done.8
  13.5 0.6 %coefficients.1 = (f32[64,32,128]{2,1,0:T(8,128)S(1)}, f32[64,32,128]{2,1,0:T(8,128)S(1)}) custom-call(f32[32,128]{1,0:T(8,128)S(1)} %copy-done.8), custom_call_target="tpu_custom_call" | custom-call | bytes 160000 | tf_op jit(solution)/shard_map/coefficients/pallas_call | solution.py:364
  14.1 0.0 copy-done.2
  14.1 0.0 copy-done.6
  14.1 0.0 copy-done.7
  14.1 0.7 %parents.1 = (f32[8,8,128]{2,1,0:T(8,128)S(1)}, f32[8,40,128]{2,1,0:T(8,128)S(1)}) custom-call(f32[3,3,64,128]{3,2,1,0:T(8,128)S(1)} %bitcast.3, f32[3,3,32,64]{3,2,1,0:T(8,128)S(1)} %bitcast.7, f32[3,3,3,64]{3,2,1,0:T(4,128)S(1)} %bitcast.8), custom_call_target="tpu_custom_call" | custom-call | bytes 160000 | tf_op jit(solution)/shard_map/parents/pallas_call | solution.py:364
  14.8 4.3 %collective-permute-done.3.rest_4_ = f32[12,32,128]{2,1,0:T(8,128)S(1)} collective-permute-done((f32[12,32,128]{2,1,0:T(8,128)S(1)}, f32[12,32,128]{2,1,0:T(8,128)S(1)}, u32[]{:S(2)}, u32[]{:S(2)}) %collective-permute-start.3) | collective-permute-done | bytes 196640 | tf_op jit(solution)/shard_map/ppermute | solution.py:398
  19.1 0.0 collective-permute-done.2.rest_3_
  19.1 0.0 copy-done.1
  19.1 0.0 copy-done.4
  19.1 2.1 %inner1.1 = (f32[64,32,128]{2,1,0:T(8,128)S(1)}, f32[64,48,128]{2,1,0:T(8,128)S(1)}, f32[64,32,128]{2,1,0:T(8,128)S(1)}, f32[64,32,128]{2,1,0:T(8,128)S(1)}, f32[64,16,128]{2,1,0:T(8,128)S(1)}) custom-call(f32[64,32,128]{2,1,0:T(8,128)S(1)} %copy-done, f32[64,32,128]{2,1,0:T(8,128)S(1)} %copy-done.1, f32[64,32,128]{2,1,0:T(8,128)S(1)} %copy-done.3, ...), custom_call_target="tpu_custom_call" | custom-call | bytes 960000 | tf_op jit(solution)/shard_map/inner1/pallas_call | solution.py:364
  21.2 0.0 collective-permute-done.1.x2
  21.2 0.0 collective-permute-done.x1
  21.2 1.0 %outer1.1 = (f32[64,32,128]{2,1,0:T(8,128)S(1)}, f32[64,48,128]{2,1,0:T(8,128)S(1)}, f32[384,128]{1,0:T(8,128)S(1)}, f32[384,128]{1,0:T(8,128)S(1)}) custom-call(f32[576,128]{1,0:T(8,128)S(1)} %collective-permute-done.x1, f32[576,128]{1,0:T(8,128)S(1)} %collective-permute-done.1.x2, ...), custom_call_target="tpu_custom_call", output_to_operand_aliasing={{0}: (7, {}), {1}: (8, {})} | custom-call | bytes 160000 | tf_op jit(solution)/shard_map/outer1/pallas_call | solution.py:364
  22.2 1.5 %collective-permute-start.4 = (f32[384,128]{1,0:T(8,128)S(1)}, f32[384,128]{1,0:T(8,128)S(1)}, u32[]{:S(2)}, u32[]{:S(2)}) collective-permute-start(f32[384,128]{1,0:T(8,128)S(1)} %get-tuple-element.40), channel_id=1, source_target_pairs={{0,16},{16,0},{32,48},{48,32},{64,80},{80,64},{96,112},{112,96},{1... | collective-permute-start | bytes 589832 | tf_op jit(solution)/shard_map/ppermute | solution.py:428
  23.7 3.7 %collective-permute-start.5 = (f32[384,128]{1,0:T(8,128)S(1)}, f32[384,128]{1,0:T(8,128)S(1)}, u32[]{:S(2)}, u32[]{:S(2)}) collective-permute-start(f32[384,128]{1,0:T(8,128)S(1)} %get-tuple-element.41), channel_id=1, source_target_pairs={{0,0},{16,32},{32,16},{48,64},{64,48},{80,96},{96,80},{112,112},{1... | collective-permute-start | bytes 589832 | tf_op jit(solution)/shard_map/ppermute | solution.py:427
  27.5 0.3 y_pack.1
  27.8 5.1 %collective-permute-start.7 = (f32[8,32,128]{2,1,0:T(8,128)S(1)}, f32[8,32,128]{2,1,0:T(8,128)S(1)}, u32[]{:S(2)}, u32[]{:S(2)}) collective-permute-start(f32[8,32,128]{2,1,0:T(8,128)S(1)} %y_pack.1), channel_id=1, source_target_pairs={{0,0},{1,2},{2,1},{3,4},{4,3},{5,6},{6,5},{7,8},{8,7},{9,10},{10,9... | collective-permute-start | bytes 393224 | tf_op jit(solution)/shard_map/ppermute | solution.py:431
  32.9 0.1 collective-permute-start.6
  33.0 4.2 %collective-permute-done.7.rest_5_ = f32[8,32,128]{2,1,0:T(8,128)S(1)} collective-permute-done((f32[8,32,128]{2,1,0:T(8,128)S(1)}, f32[8,32,128]{2,1,0:T(8,128)S(1)}, u32[]{:S(2)}, u32[]{:S(2)}) %collective-permute-start.7) | collective-permute-done | bytes 131104 | tf_op jit(solution)/shard_map/ppermute | solution.py:431
  37.2 0.0 collective-permute-done.6.rest_4_
  37.2 2.1 %inner2.1 = (f32[64,32,128]{2,1,0:T(8,128)S(1)}, f32[64,48,128]{2,1,0:T(8,128)S(1)}, f32[64,32,128]{2,1,0:T(8,128)S(1)}, f32[64,16,128]{2,1,0:T(8,128)S(1)}) custom-call(f32[64,32,128]{2,1,0:T(8,128)S(1)} %get-tuple-element.42.p, f32[64,48,128]{2,1,0:T(8,128)S(1)} %get-tuple-element.43.u, f32[64,32,128]{2,1,0:T(8,128)S(1)} %get-tuple-element.44.v, ...), custom_call_target="tpu_custom_call" | custom-call | bytes 960000 | tf_op jit(solution)/shard_map/inner2/pallas_call | solution.py:364
  39.4 0.0 collective-permute-done.4.x1
  39.4 0.0 collective-permute-done.5.x2
  39.4 0.9 %outer2.1 = (f32[64,32,128]{2,1,0:T(8,128)S(1)}, f32[64,48,128]{2,1,0:T(8,128)S(1)}, f32[384,128]{1,0:T(8,128)S(1)}) custom-call(f32[384,128]{1,0:T(8,128)S(1)} %collective-permute-done.4.x1, f32[384,128]{1,0:T(8,128)S(1)} %collective-permute-done.5.x2, f32[64,32,128]{2,1,0:T(8,128)S(1)} %get-tuple-element.42.p, ...), custom_call_target="tpu_custom_call", output_to_operand_aliasing={{0}: (7, {}), {1}: (8, {})} | custom-call | bytes 160000 | tf_op jit(solution)/shard_map/outer2/pallas_call | solution.py:364
  40.3 0.1 collective-permute-start.8
  40.4 0.0 copy-start.9
  40.4 0.9 %north_pack.1 = (f32[8,32,128]{2,1,0:T(8,128)S(1)}, f32[8,8,128]{2,1,0:T(8,128)S(1)}) custom-call(f32[64,48,128]{2,1,0:T(8,128)S(1)} %get-tuple-element.50.u, f32[64,32,128]{2,1,0:T(8,128)S(1)} %get-tuple-element.49.tail_0_.v, f32[64,32,128]{2,1,0:T(8,128)S(1)} %get-tuple-element.51.p, f32[8,8,128]{2,1,0:T(8,128)S(1)} %get-tuple-element.35.rest_5_.pe, ...), custom_call_target="tpu_custom_call" | custom-call | bytes 160000 | tf_op jit(solution)/shard_map/north_pack/pallas_call | solution.py:364
  41.3 0.1 collective-permute-start.9
  41.4 0.1 collective-permute-start.10
  41.4 0.0 copy-done.9
  41.4 1.5 %turn.1 = (f32[64,32,128]{2,1,0:T(8,128)S(1)}, f32[64,32,128]{2,1,0:T(8,128)S(1)}, f32[64,32,128]{2,1,0:T(8,128)S(1)}, f32[512,128]{1,0:T(8,128)S(1)}) custom-call(s32[2]{0:T(128)S(1)} %copy-done.9, f32[64,48,128]{2,1,0:T(8,128)S(1)} %get-tuple-element.50.u, f32[64,32,128]{2,1,0:T(8,128)S(1)} %get-tuple-element.49.tail_0_.v, ...), custom_call_target="tpu_custom_call" | custom-call | bytes 160000 | tf_op jit(solution)/shard_map/turn/pallas_call | solution.py:364
  42.9 9.7 %collective-permute-done.10.corner = f32[8,8,128]{2,1,0:T(8,128)S(1)} collective-permute-done((f32[8,8,128]{2,1,0:T(8,128)S(1)}, f32[8,8,128]{2,1,0:T(8,128)S(1)}, u32[]{:S(2)}, u32[]{:S(2)}) %collective-permute-start.10) | collective-permute-done | bytes 32800 | tf_op jit(solution)/shard_map/ppermute | solution.py:459
  52.7 0.0 collective-permute-done.9.north
  52.7 0.0 collective-permute-done.8.east
  52.7 2.7 %move.1 = (f32[64,32,128]{2,1,0:T(8,128)}, f32[64,32,128]{2,1,0:T(8,128)}, f32[64,32,128]{2,1,0:T(8,128)}) custom-call(s32[2]{0:T(128)S(1)} %copy-done.9, f32[64,32,128]{2,1,0:T(8,128)S(1)} %get-tuple-element.52.ru, f32[64,32,128]{2,1,0:T(8,128)S(1)} %get-tuple-element.53.rv, f32[64,32,128]{2,1,0:T(8,128)S(1)} %get-tuple-element.54.rp, ...), custom_call_target="tpu_custom_call" | custom-call | bytes 160000 | tf_op jit(solution)/shard_map/move/pallas_call | solution.py:364
Async XLA Ops:
  0.6 7.7 %copy-start = (f32[64,32,128]{2,1,0:T(8,128)S(1)}, f32[64,32,128]{2,1,0:T(8,128)}, u32[]{:S(2)}) copy-start(f32[64,32,128]{2,1,0:T(8,128)} %p.7) | copy-start | bytes 3145732
  0.6 7.7 %copy-start.3 = (f32[64,32,128]{2,1,0:T(8,128)S(1)}, f32[64,32,128]{2,1,0:T(8,128)}, u32[]{:S(2)}) copy-start(f32[64,32,128]{2,1,0:T(8,128)} %v.3) | copy-start | bytes 3145732
  2.9 11.1 %copy-start.2 = (f32[3,64,3,128]{3,1,2,0:T(8,128)S(1)}, f32[3,64,3,128]{3,1,2,0:T(8,128)}, u32[]{:S(2)}) copy-start(f32[3,64,3,128]{3,1,2,0:T(8,128)} %param.13) | copy-start | bytes 884740
  3.0 16.1 %copy-start.1 = (f32[64,32,128]{2,1,0:T(8,128)S(1)}, f32[64,32,128]{2,1,0:T(8,128)}, u32[]{:S(2)}) copy-start(f32[64,32,128]{2,1,0:T(8,128)} %u.5) | copy-start | bytes 3145732
  3.0 16.1 %copy-start.4 = (bf16[256,256]{1,0:T(8,128)(2,1)S(1)}, bf16[256,256]{1,0:T(8,128)(2,1)}, u32[]{:S(2)}) copy-start(bf16[256,256]{1,0:T(8,128)(2,1)} %constant.2.clone.rest_2_.rest_3_) | copy-start | bytes 393220
  3.0 18.2 %collective-permute-start.1 = (f32[576,128]{1,0:T(8,128)}, f32[576,128]{1,0:T(8,128)S(1)}, u32[]{:S(2)}, u32[]{:S(2)}) collective-permute-start(f32[576,128]{1,0:T(8,128)} %get-tuple-element.32), channel_id=1, source_target_pairs={{0,0},{16,32},{32,16},{48,64},{64,48},{80,96},{96,80},{112,112},{1... | collective-permute-start | bytes 884744 | tf_op jit(solution)/shard_map/ppermute | solution.py:394
  8.3 12.9 %collective-permute-start = (f32[576,128]{1,0:T(8,128)}, f32[576,128]{1,0:T(8,128)S(1)}, u32[]{:S(2)}, u32[]{:S(2)}) collective-permute-start(f32[576,128]{1,0:T(8,128)} %get-tuple-element.31.after), channel_id=1, source_target_pairs={{0,16},{16,0},{32,48},{48,32},{64,80},{80,64},{96,112},{112,96},{1... | collective-permute-start | bytes 884744 | tf_op jit(solution)/shard_map/ppermute | solution.py:395
  8.4 1.0 %copy-start.5 = (f32[576,128]{1,0:T(8,128)S(1)}, f32[576,128]{1,0:T(8,128)}, u32[]{:S(2)}) copy-start(f32[576,128]{1,0:T(8,128)} %get-tuple-element.31.after) | copy-start | bytes 884740
  9.4 4.1 %copy-start.8 = (f32[32,128]{1,0:T(8,128)S(1)}, f32[32,128]{1,0:T(8,128)}, u32[]{:S(2)}) copy-start(f32[32,128]{1,0:T(8,128)} %s_ref.1) | copy-start | bytes 49156
  9.4 4.7 %copy-start.6 = (f32[3,64,32,3]{1,2,3,0:T(8,128)S(1)}, f32[3,64,32,3]{1,2,3,0:T(8,128)}, u32[]{:S(2)}) copy-start(f32[3,64,32,3]{1,2,3,0:T(8,128)} %param.14) | copy-start | bytes 221188
  9.4 4.7 %copy-start.7 = (f32[3,64,3,3]{1,3,2,0:T(4,128)S(1)}, f32[3,64,3,3]{1,3,2,0:T(4,128)}, u32[]{:S(2)}) copy-start(f32[3,64,3,3]{1,3,2,0:T(4,128)} %param.15) | copy-start | bytes 20740
  10.0 9.1 %collective-permute-start.3 = (f32[12,32,128]{2,1,0:T(8,128)S(1)}, f32[12,32,128]{2,1,0:T(8,128)S(1)}, u32[]{:S(2)}, u32[]{:S(2)}) collective-permute-start(f32[12,32,128]{2,1,0:T(8,128)S(1)} %y_edges.1), channel_id=1, source_target_pairs={{0,0},{1,2},{2,1},{3,4},{4,3},{5,6},{6,5},{7,8},{8,7},{9,10},{10,9... | collective-permute-start | bytes 589832 | tf_op jit(solution)/shard_map/ppermute | solution.py:398
  13.4 5.7 %collective-permute-start.2 = (f32[12,32,128]{2,1,0:T(8,128)S(1)}, f32[12,32,128]{2,1,0:T(8,128)S(1)}, u32[]{:S(2)}, u32[]{:S(2)}) collective-permute-start(f32[12,32,128]{2,1,0:T(8,128)S(1)} %y_edges.1), channel_id=1, source_target_pairs={{0,1},{1,0},{2,3},{3,2},{4,5},{5,4},{6,7},{7,6},{8,9},{9,8},{10,11... | collective-permute-start | bytes 589832 | tf_op jit(solution)/shard_map/ppermute | solution.py:397
  22.2 17.2 %collective-permute-start.4 = (f32[384,128]{1,0:T(8,128)S(1)}, f32[384,128]{1,0:T(8,128)S(1)}, u32[]{:S(2)}, u32[]{:S(2)}) collective-permute-start(f32[384,128]{1,0:T(8,128)S(1)} %get-tuple-element.40), channel_id=1, source_target_pairs={{0,16},{16,0},{32,48},{48,32},{64,80},{80,64},{96,112},{112,96},{1... | collective-permute-start | bytes 589832 | tf_op jit(solution)/shard_map/ppermute | solution.py:428
  23.7 15.6 %collective-permute-start.5 = (f32[384,128]{1,0:T(8,128)S(1)}, f32[384,128]{1,0:T(8,128)S(1)}, u32[]{:S(2)}, u32[]{:S(2)}) collective-permute-start(f32[384,128]{1,0:T(8,128)S(1)} %get-tuple-element.41), channel_id=1, source_target_pairs={{0,0},{16,32},{32,16},{48,64},{64,48},{80,96},{96,80},{112,112},{1... | collective-permute-start | bytes 589832 | tf_op jit(solution)/shard_map/ppermute | solution.py:427
  27.8 9.5 %collective-permute-start.7 = (f32[8,32,128]{2,1,0:T(8,128)S(1)}, f32[8,32,128]{2,1,0:T(8,128)S(1)}, u32[]{:S(2)}, u32[]{:S(2)}) collective-permute-start(f32[8,32,128]{2,1,0:T(8,128)S(1)} %y_pack.1), channel_id=1, source_target_pairs={{0,0},{1,2},{2,1},{3,4},{4,3},{5,6},{6,5},{7,8},{8,7},{9,10},{10,9... | collective-permute-start | bytes 393224 | tf_op jit(solution)/shard_map/ppermute | solution.py:431
  32.9 4.3 %collective-permute-start.6 = (f32[8,32,128]{2,1,0:T(8,128)S(1)}, f32[8,32,128]{2,1,0:T(8,128)S(1)}, u32[]{:S(2)}, u32[]{:S(2)}) collective-permute-start(f32[8,32,128]{2,1,0:T(8,128)S(1)} %y_pack.1), channel_id=1, source_target_pairs={{0,1},{1,0},{2,3},{3,2},{4,5},{5,4},{6,7},{7,6},{8,9},{9,8},{10,11... | collective-permute-start | bytes 393224 | tf_op jit(solution)/shard_map/ppermute | solution.py:430
  40.3 12.4 %collective-permute-start.8 = (f32[384,128]{1,0:T(8,128)S(1)}, f32[384,128]{1,0:T(8,128)S(1)}, u32[]{:S(2)}, u32[]{:S(2)}) collective-permute-start(f32[384,128]{1,0:T(8,128)S(1)} %get-tuple-element.56), channel_id=1, source_target_pairs={{0,112},{16,0},{32,16},{48,32},{64,48},{80,64},{96,80},{112,96},{1... | collective-permute-start | bytes 589832 | tf_op jit(solution)/shard_map/ppermute | solution.py:451
  40.4 1.1 %copy-start.9 = (s32[2]{0:T(128)S(1)}, s32[2]{0:T(128)}, u32[]{:S(2)}) copy-start(s32[2]{0:T(128)} %offsets.3) | copy-start | bytes 28
  41.3 11.4 %collective-permute-start.9 = (f32[8,32,128]{2,1,0:T(8,128)S(1)}, f32[8,32,128]{2,1,0:T(8,128)S(1)}, u32[]{:S(2)}, u32[]{:S(2)}) collective-permute-start(f32[8,32,128]{2,1,0:T(8,128)S(1)} %get-tuple-element.57), channel_id=1, source_target_pairs={{0,15},{1,0},{2,1},{3,2},{4,3},{5,4},{6,5},{7,6},{8,7},{9,8},{10,9... | collective-permute-start | bytes 393224 | tf_op jit(solution)/shard_map/ppermute | solution.py:458
  41.4 11.3 %collective-permute-start.10 = (f32[8,8,128]{2,1,0:T(8,128)S(1)}, f32[8,8,128]{2,1,0:T(8,128)S(1)}, u32[]{:S(2)}, u32[]{:S(2)}) collective-permute-start(f32[8,8,128]{2,1,0:T(8,128)S(1)} %get-tuple-element.58), channel_id=1, source_target_pairs={{0,127},{1,112},{2,113},{3,114},{4,115},{5,116},{6,117},{7,118},{8... | collective-permute-start | bytes 98312 | tf_op jit(solution)/shard_map/ppermute | solution.py:459

commit v2 on v1

--- a/solution.py
+++ b/solution.py
@@ -26,7 +26,7 @@
 
 def swaps(count):
     inner = [(i, i ^ 1) for i in range(count)]
-    outer = [(i, min(max(((i + 1) ^ 1) - 1, 0), count - 1)) for i in range(count)]
+    outer = [(i, (i + 1) % count if i % 2 else (i - 1) % count) for i in range(count)]
     return inner, outer
 
 
@@ -46,12 +46,19 @@
     )
 
 
-def pack(rows, width, step, lanes):
-    out = None
-    for m, row in enumerate(rows):
-        moved = roll_lanes(row, m * step + width)
-        out = moved if out is None else jnp.where(lanes >= m * step, moved, out)
-    return out
+def pack_edges(rows, step, lanes):
+    moved = [roll_lanes(row, m * step) for m, row in enumerate(rows)]
+    low = high = moved[0]
+    for m in range(1, len(moved)):
+        low = jnp.where(lanes >= m * step, moved[m], low)
+    for m in range(len(moved) - 1, 0, -1):
+        high = jnp.where(lanes < m * step, moved[m], high)
+    return low, high
+
+
+def unpack_edges(north, south, m, step, lanes):
+    mine = jnp.logical_and(lanes >= m * step, lanes < (m + 1) * step)
+    return roll_lanes(jnp.where(mine, north, south), -m * step)
 
 
 def write_edges(buffers, east, first, second):
@@ -86,18 +93,22 @@
     write_edges((((pw, 6), (uw, 3)), ((pe, 6), (ue, 3))), even, first, second)
 
 
-def y_edges_kernel(p, v, after, out):
+def write_y_edges(field, count, step, at, first, second):
     lanes = lane_index()
-    for b in range(8):
-        out[b] = pack([p[8 * b + m] for m in range(8)], 6, 16, lanes)
-    for b in range(4):
-        out[8 + b] = pack([v[16 * b + m] for m in range(16)], 3, 8, lanes)
-
-
-def y_pack_kernel(p, out):
-    lanes = lane_index()
-    for b in range(8):
-        out[b] = pack([p[8 * b + m] for m in range(8)], 6, 16, lanes)
+    even = lax.axis_index("gy") % 2 == 0
+    for b in range(64 // count):
+        low, high = pack_edges([field[count * b + m] for m in range(count)], step, lanes)
+        first[at + b] = jnp.where(even, high, low)
+        second[at + b] = jnp.where(even, low, high)
+
+
+def y_edges_kernel(p, v, first, second):
+    write_y_edges(p, 16, 8, 0, first, second)
+    write_y_edges(v, 32, 4, 4, first, second)
+
+
+def y_pack_kernel(p, first, second):
+    write_y_edges(p, 16, 8, 0, first, second)
 
 
 def coefficients_kernel(s_ref, inv_ref, g_ref):
@@ -130,13 +141,19 @@
             out[pl.ds(x, 64, stride=3), :] = pe[f, x]
 
 
-def inner_kernel(first_step, p, u, v, *rest):
+def across_kernel(first_step, p, u, u_out, ex_out):
+    du = 0 if first_step else 8
+    for l in range(64):
+        step = difference(lambda k: p[l, 5 + k : 29 + k, :])
+        u_out[l, 13:37, :] = u[l, du + 5 : du + 29, :] - step
+        ex_out[l] = difference(lambda k: u_out[l, 16 + k : 32 + k, :])
+
+
+def inner_kernel(first_step, p, v, ex, *rest):
     if first_step:
-        inv, g, mat, y1, y2, keep1, keep2, keep3, p_out, u_out, v_out, vh_out, rest_out, w_buf = rest
-        du = 0
+        inv, g, mat, y1, y2, keep1, keep2, keep3, p_out, v_out, vh_out, rest_out, w_buf = rest
     else:
-        vh_in, inv, g, mat, y1, y2, p_out, u_out, v_out, rest_out, w_buf = rest
-        du = 8
+        vh_in, inv, g, mat, y1, y2, p_out, v_out, rest_out, w_buf = rest
     lanes = lane_index()
     gy = lax.axis_index("gy")
     even_y = gy % 2 == 0
@@ -144,20 +161,21 @@
     in_n = gy < lax.axis_size("gy") - 1
     lane_ok = jnp.where(lanes < 64, jnp.where(in_n, 1.0, 0.0), jnp.where(in_s, 1.0, 0.0))
 
-    def sides(b, low):
-        a, c = y1[b], y2[b]
-        north = jnp.where(in_n, jnp.where(even_y, a, c), 0.0)
-        south = jnp.where(in_s, jnp.where(even_y, c, a), 0.0)
-        return jnp.where(low, south, north)
+    def halos(at, levels, count, step):
+        out = []
+        for l in levels:
+            a, c = y1[at + l // count], y2[at + l // count]
+            north = jnp.where(in_n, jnp.where(even_y, a, c), 0.0)
+            south = jnp.where(in_s, jnp.where(even_y, c, a), 0.0)
+            out.append(unpack_edges(north, south, l % count, step, lanes))
+        return jnp.concatenate(out, axis=0)
 
     w = jnp.zeros((16, 128), F32)
     for b in range(8):
-        blk = sides(b, lanes % 16 < 6)
-        halo = jnp.concatenate([roll_lanes(blk, -(16 * m + 6)) for m in range(8)], axis=0)
+        levels = range(8 * b, 8 * b + 8)
+        halo = halos(0, levels, 16, 8)
         if first_step:
-            blk = sides(8 + b // 2, lanes % 8 < 3)
-            at = 64 * (b % 2) + 3
-            vh = jnp.concatenate([roll_lanes(blk, -(at + 8 * m)) for m in range(8)], axis=0)
+            vh = halos(4, levels, 32, 4)
         else:
             vh = vh_in[8 * b : 8 * b + 8].reshape(256, 128)
         own = p[8 * b : 8 * b + 8].reshape(256, 128)
@@ -174,10 +192,7 @@
             row = left[32 * m : 32 * m + 32]
             rest_out[l, 0:8, :] = row[0:8]
             rest_out[l, 8:16, :] = row[24:32]
-            step = difference(lambda k: p[l, 5 + k : 29 + k, :])
-            u_out[l, 13:37, :] = u[l, du + 5 : du + 29, :] - step
-            rhs = row[8:24] - difference(lambda k: u_out[l, 16 + k : 32 + k, :])
-            w = rhs * inv[l, 8:24, :] + g[l, 8:24, :] * w
+            w = (row[8:24] - ex[l]) * inv[l, 8:24, :] + g[l, 8:24, :] * w
             w_buf[l] = w
     q = jnp.zeros((16, 128), F32)
     for l in range(63, -1, -1):
@@ -281,43 +296,60 @@
         pn_strip[b] = strip
 
 
-def north_pack_kernel(u, v, p, pe, pn, out, out_corner):
+def strip_of(fields, b, lanes):
+    strip = None
+    for m in range(8):
+        for f, field in enumerate(fields):
+            moved = roll_lanes(field(8 * b + m), 16 * m + 3 * f)
+            strip = moved if strip is None else jnp.where(lanes >= 16 * m + 3 * f, moved, strip)
+    return strip
+
+
+def corner_pack_kernel(u, v, p, pe, pn, out):
     lanes = lane_index()
     west = lax.axis_index("gx") == 0
     south = lax.axis_index("gy") == 0
+    fields = (lambda l: u[l, 8:16, :], lambda l: v[l, 0:8, :], lambda l: p[l, 0:8, :])
     for b in range(8):
-        strip = None
-        for m in range(8):
-            l = 8 * b + m
-            for f, val in enumerate((u[l, 8:40, :], v[l], p[l])):
-                at = 16 * m + 3 * f
-                moved = roll_lanes(val, at)
-                strip = moved if strip is None else jnp.where(lanes >= at, moved, strip)
-        out[b] = jnp.where(south, pn[b, 0:32, :], strip)
         edge = jnp.where(west, pn[b, 32:40, :], pn[b, 0:8, :])
-        out_corner[b] = jnp.where(south, edge, jnp.where(west, pe[b], strip[0:8]))
-
-
-def turn_kernel(offsets, u, v, p, pe, ru, rv, rp, tail):
+        strip = strip_of(fields, b, lanes)
+        out[b] = jnp.where(south, edge, jnp.where(west, pe[b], strip))
+
+
+def north_pack_kernel(u, v, p, pn, after, out):
+    lanes = lane_index()
+    south = lax.axis_index("gy") == 0
+    fields = (lambda l: u[l, 8:40, :], lambda l: v[l], lambda l: p[l])
+    for b in range(8):
+        out[b] = jnp.where(south, pn[b, 0:32, :], strip_of(fields, b, lanes))
+
+
+def turn_kernel(offsets, u, v, p, pe, ru, rv, rp, tu, tv, tp):
+    o0 = offsets[0]
     shift = lax.rem(128 - offsets[1], 128)
     for l in range(64):
-        ru[l] = pltpu.roll(u[l, 8:40, :], shift, 1)
-        rv[l] = pltpu.roll(v[l], shift, 1)
-        rp[l] = pltpu.roll(p[l], shift, 1)
-        tail[8 * l : 8 * l + 8, :] = pltpu.roll(u[l, 40:48, :], shift, 1)
+        tu[40 * l : 40 * l + 40, :] = pltpu.roll(u[l, 8:48, :], shift, 1)
+        tv[40 * l : 40 * l + 32, :] = pltpu.roll(v[l], shift, 1)
+        tp[40 * l : 40 * l + 32, :] = pltpu.roll(p[l], shift, 1)
 
     @pl.when(lax.axis_index("gx") == lax.axis_size("gx") - 1)
     def _():
         for x in range(3):
-            tail[pl.ds(x, 64, stride=8), :] = pltpu.roll(pe[0, x], shift, 1)
-
-
-def move_kernel(offsets, ru, rv, rp, tail, east, north, corner, ou, ov, op, bu, bv, bp, ext, ns, columns, sems):
+            tu[pl.ds(32 + x, 64, stride=40), :] = pltpu.roll(pe[0, x], shift, 1)
+
+    for l in range(64):
+        ru[l] = tu[pl.ds(40 * l + o0, 32), :]
+        rv[l] = tv[pl.ds(40 * l + o0, 32), :]
+        rp[l] = tp[pl.ds(40 * l + o0, 32), :]
+
+
+def move_kernel(offsets, ru, rv, rp, east, north, corner, ou, ov, op, bu, bv, bp, ns, columns, sems):
     lanes = lane_index()
     o0, o1 = offsets[0], offsets[1]
     own_lane = lanes < 128 - o1
+    own_row = lax.broadcasted_iota(jnp.int32, (8, 128), 0) < 8 - o0
     shift = lax.rem(128 - o1, 128)
-    columns[...] = pltpu.roll(east[...], shift, 1)
+    columns[8:392, :] = pltpu.roll(east[...], shift, 1)
     copies = []
     for b in range(8):
         ns[b, 0:32, :] = north[b]
@@ -326,16 +358,14 @@
         for m in range(8):
             l = 8 * b + m
             for f, (src, buf) in enumerate(((ru, bu), (rv, bv), (rp, bp))):
-                ext[f, l, 0:8, :] = src[l, 24:32, :]
-                if f == 0:
-                    ext[f, l, 8:16, :] = tail[8 * l : 8 * l + 8, :]
-                else:
-                    at = 192 * (f - 1) + 3 * l
-                    ext[f, l, 8:11, :] = columns[at : at + 3, :]
                 back = lax.rem(256 - (16 * m + 3 * f) - o1, 128)
                 strip = pltpu.roll(nrow, back, 1)
-                buf[l, 0:24, :] = jnp.where(own_lane, src[l, pl.ds(o0, 24), :], strip[0:24])
-                buf[l, 24:32, :] = jnp.where(own_lane, ext[f, l, pl.ds(o0, 8), :], strip[24:32])
+                buf[l, 0:24, :] = jnp.where(own_lane, src[l, 0:24, :], strip[0:24])
+                last = src[l, 24:32, :]
+                if f > 0:
+                    new = columns[pl.ds(192 * (f - 1) + 3 * l + o0, 8), :]
+                    last = jnp.where(own_row, last, new)
+                buf[l, 24:32, :] = jnp.where(own_lane, last, strip[24:32])
         for f, (buf, out) in enumerate(((bu, ou), (bv, ov), (bp, op))):
             part = pl.ds(8 * b, 8)
             copy = pltpu.make_async_copy(buf.at[part], out.at[part], sems.at[8 * f + b])
@@ -393,9 +423,11 @@
     )
     x2 = lax.ppermute(second, "gx", x_out)
     x1 = lax.ppermute(first, "gx", x_in)
-    strip = call(y_edges_kernel, sds(12, 32, 128), (pressure, wind_north, first), name="y_edges", specs={2: ANY})
-    y1 = lax.ppermute(strip, "gy", y_in)
-    y2 = lax.ppermute(strip, "gy", y_out)
+    first, second = call(
+        y_edges_kernel, (sds(6, 32, 128), sds(6, 32, 128)), (pressure, wind_north), name="y_edges"
+    )
+    y1 = lax.ppermute(first, "gy", y_in)
+    y2 = lax.ppermute(second, "gy", y_out)
     inv, g = call(coefficients_kernel, (field, field), (stiffness,), name="coefficients")
 
     pe = parent_east.transpose(0, 2, 1, 3)
@@ -407,10 +439,13 @@
         name="parents",
     )
 
-    p1, u1, v1, vh1, rest = call(
+    u1, ex = call(
+        functools.partial(across_kernel, True), (padded, outer), (pressure, wind_east), name="across1"
+    )
+    p1, v1, vh1, rest = call(
         functools.partial(inner_kernel, True),
-        (field, padded, field, field, outer),
-        (pressure, wind_east, wind_north, inv, g, mat, y1, y2, pe_strip, pn_strip, pe),
+        (field, field, field, outer),
+        (pressure, wind_north, ex, inv, g, mat, y1, y2, pe_strip, pn_strip, pe),
         buffers((64, 16, 128)),
         name="inner1",
         specs={8: ANY, 9: ANY, 10: ANY},
@@ -426,13 +461,18 @@
     )
     x2 = lax.ppermute(second, "gx", x_out)
     x1 = lax.ppermute(first, "gx", x_in)
-    strip = call(y_pack_kernel, sds(8, 32, 128), (p1,), name="y_pack")
-    y1 = lax.ppermute(strip, "gy", y_in)
-    y2 = lax.ppermute(strip, "gy", y_out)
-    p2, u2, v2, rest = call(
+    first, second = call(
+        y_pack_kernel, (sds(4, 32, 128), sds(4, 32, 128)), (p1,), name="y_pack"
+    )
+    y1 = lax.ppermute(first, "gy", y_in)
+    y2 = lax.ppermute(second, "gy", y_out)
+    u2, ex = call(
+        functools.partial(across_kernel, False), (padded, outer), (p1, u1), name="across2"
+    )
+    p2, v2, rest = call(
         functools.partial(inner_kernel, False),
-        (field, padded, field, outer),
-        (p1, u1, v1, vh1, inv, g, mat, y1, y2),
+        (field, field, outer),
+        (p1, v1, ex, vh1, inv, g, mat, y1, y2),
         buffers((64, 16, 128)),
         name="inner2",
         us=0.3,
@@ -449,26 +489,27 @@
         alias={7: 0, 8: 1},
     )
     east = lax.ppermute(east, "gx", down_x)
-    north, corner = call(
-        north_pack_kernel,
-        (sds(8, 32, 128), sds(8, 8, 128)),
-        (u2, v2, p2, pe_strip, pn_strip),
-        name="north_pack",
+    corner = call(
+        corner_pack_kernel, sds(8, 8, 128), (u2, v2, p2, pe_strip, pn_strip), name="corner_pack"
+    )
+    from_corner = lax.ppermute(corner, ("gx", "gy"), down)
+    north = call(
+        north_pack_kernel, sds(8, 32, 128), (u2, v2, p2, pn_strip, corner), name="north_pack"
     )
     north = lax.ppermute(north, "gy", down_y)
-    corner = lax.ppermute(corner, ("gx", "gy"), down)
-    ru, rv, rp, tail = call(
+    ru, rv, rp = call(
         turn_kernel,
-        (field, field, field, sds(512, 128)),
+        (field, field, field),
         (offsets, u2, v2, p2, pe),
+        buffers(*[(64 * 40, 128)] * 3),
         name="turn",
         specs={0: SMEM},
     )
     return call(
         move_kernel,
         (field, field, field),
-        (offsets, ru, rv, rp, tail, east, north, corner),
-        buffers(*[(64, 32, 128)] * 3, (3, 64, 16, 128), (8, 40, 128), (384, 128))
+        (offsets, ru, rv, rp, east, north, from_corner),
+        buffers(*[(64, 32, 128)] * 3, (8, 40, 128), (392, 128))
         + [dma((24,))],
         name="move",
         specs={0: SMEM},

time: 55.6 us -> 47.9 us (0.86)
  starting transfers between devices: 19.6 us -> 11.3 us
  Pallas kernels: 15.7 us -> 16.7 us
  local copies, waits for them, and re-layouts: 1.01 us -> 0.05 us
    ppermute x5, starting transfers between devices: 8.79 us -> 5.03 us  [the longest x2 3.69 us: on_device(): y1 = lax.ppermute(first, 'gy', y_in)]
    ppermute x2, starting transfers between devices: 9.02 us -> 5.32 us  [on_device(): x2 = lax.ppermute(second, 'gx', x_out)]
    pallas_call x12 -> x15, Pallas kernels: 15.7 us -> 16.7 us  [call(): pl.pallas_call(body, out_shape=out_shape, in_specs=[specs.get(k, VMEM) fo...]
    ppermute x2, starting transfers between devices: 1.62 us -> 0.63 us  [on_device(): x1 = lax.ppermute(first, 'gx', x_in)]
    unnamed x20 -> x18, local copies, waits for them, and re-layouts: 1.01 us -> 0.05 us
  transfers between devices with their start and end apart: 11 -> 11, of which waited for: 3 -> 3; matrix products, arithmetic and copies ran while one was open for 0% -> 0% of each run, Pallas kernels for 16% -> 21%
where the time goes in v2:
time: 47.9 us; the launch traced here: 47.5 us
  waiting for transfers between devices  18.4 us (38%)
  Pallas kernels  16.7 us (35%)
  starting transfers between devices  11.3 us (24%)
  between operations  1.07 us (2%)
    pallas_call x15, Pallas kernels, call(): pl.pallas_call(body, out_shape=out_shape, in_specs=[specs.get(k, VMEM) fo...  16.7 us
    ppermute x2, waiting for transfers between devices, on_device(): y2 = lax.ppermute(second, 'gy', y_out)  9.3 us
    ppermute x1, waiting for transfers between devices, on_device(): from_corner = lax.ppermute(corner, ('gx', 'gy'), down)  9.03 us
    ppermute x2, starting transfers between devices, on_device(): x2 = lax.ppermute(second, 'gx', x_out)  5.32 us
    ppermute x2, starting transfers between devices, on_device(): y1 = lax.ppermute(first, 'gy', y_in)  3.69 us
    ppermute x2, starting transfers between devices, on_device(): y2 = lax.ppermute(second, 'gy', y_out)  1.26 us
  transfers between devices with their start and end apart: 11, of which 3 were waited for; matrix products, arithmetic and copies ran while one was open for 0% of the time, Pallas kernels for 21%

profile of v2, /device:TPU:31, one launch (start us, length us, event | category | flops | bytes accessed | tf_op | source)
XLA Modules:
  0.0 47.5 jit_solution(12608160538406895244)
XLA Ops:
  0.6 0.0 copy-start
  0.6 0.0 copy-start.3
  0.7 2.3 %x_edges.1 = (f32[576,128]{1,0:T(8,128)}, f32[576,128]{1,0:T(8,128)}) custom-call(f32[64,32,128]{2,1,0:T(8,128)} %p.9, f32[64,32,128]{2,1,0:T(8,128)} %u.5), custom_call_target="tpu_custom_call" | custom-call | bytes 160000 | tf_op jit(solution)/shard_map/x_edges/pallas_call | solution.py:394
  2.9 0.0 copy-start.1
  3.0 0.5 %collective-permute-start = (f32[576,128]{1,0:T(8,128)}, f32[576,128]{1,0:T(8,128)S(1)}, u32[]{:S(2)}, u32[]{:S(2)}) collective-permute-start(f32[576,128]{1,0:T(8,128)} %get-tuple-element.34), channel_id=1, source_target_pairs={{0,16},{16,0},{32,48},{48,32},{64,80},{80,64},{96,112},{112,96},{1... | collective-permute-start | bytes 884744 | tf_op jit(solution)/shard_map/ppermute | solution.py:425
  3.5 4.1 %collective-permute-start.1 = (f32[576,128]{1,0:T(8,128)}, f32[576,128]{1,0:T(8,128)S(1)}, u32[]{:S(2)}, u32[]{:S(2)}) collective-permute-start(f32[576,128]{1,0:T(8,128)} %get-tuple-element.35), channel_id=1, source_target_pairs={{0,112},{16,32},{32,16},{48,64},{64,48},{80,96},{96,80},{112,0},{1... | collective-permute-start | bytes 884744 | tf_op jit(solution)/shard_map/ppermute | solution.py:424
  7.6 0.0 copy-done
  7.6 0.0 copy-done.3
  7.6 0.7 %y_edges.1 = (f32[6,32,128]{2,1,0:T(8,128)S(1)}, f32[6,32,128]{2,1,0:T(8,128)S(1)}) custom-call(f32[64,32,128]{2,1,0:T(8,128)S(1)} %copy-done, f32[64,32,128]{2,1,0:T(8,128)S(1)} %copy-done.3), custom_call_target="tpu_custom_call" | custom-call | bytes 160000 | tf_op jit(solution)/shard_map/y_edges/pallas_call | solution.py:394
  8.3 0.0 copy-start.7
  8.3 0.0 copy-start.2
  8.3 0.0 copy-start.5
  8.3 0.0 copy-start.6
  8.3 0.0 copy-start.4
  8.3 1.3 %collective-permute-start.2 = (f32[6,32,128]{2,1,0:T(8,128)S(1)}, f32[6,32,128]{2,1,0:T(8,128)S(1)}, u32[]{:S(2)}, u32[]{:S(2)}) collective-permute-start(f32[6,32,128]{2,1,0:T(8,128)S(1)} %get-tuple-element.39), channel_id=1, source_target_pairs={{0,1},{1,0},{2,3},{3,2},{4,5},{5,4},{6,7},{7,6},{8,9},{9,8},{10,11... | collective-permute-start | bytes 294920 | tf_op jit(solution)/shard_map/ppermute | solution.py:429
  9.6 0.6 %collective-permute-start.3 = (f32[6,32,128]{2,1,0:T(8,128)S(1)}, f32[6,32,128]{2,1,0:T(8,128)S(1)}, u32[]{:S(2)}, u32[]{:S(2)}) collective-permute-start(f32[6,32,128]{2,1,0:T(8,128)S(1)} %get-tuple-element.40), channel_id=1, source_target_pairs={{0,15},{1,2},{2,1},{3,4},{4,3},{5,6},{6,5},{7,8},{8,7},{9,10},{10,... | collective-permute-start | bytes 294920 | tf_op jit(solution)/shard_map/ppermute | solution.py:430
  10.3 0.0 copy-done.1
  10.3 0.6 %across1.1 = (f32[64,48,128]{2,1,0:T(8,128)S(1)}, f32[64,16,128]{2,1,0:T(8,128)S(1)}) custom-call(f32[64,32,128]{2,1,0:T(8,128)S(1)} %copy-done, f32[64,32,128]{2,1,0:T(8,128)S(1)} %copy-done.1), custom_call_target="tpu_custom_call" | custom-call | bytes 160000 | tf_op jit(solution)/shard_map/across1/pallas_call | solution.py:394
  10.9 0.0 copy-done.7
  10.9 0.6 %coefficients.1 = (f32[64,32,128]{2,1,0:T(8,128)S(1)}, f32[64,32,128]{2,1,0:T(8,128)S(1)}) custom-call(f32[32,128]{1,0:T(8,128)S(1)} %copy-done.7), custom_call_target="tpu_custom_call" | custom-call | bytes 160000 | tf_op jit(solution)/shard_map/coefficients/pallas_call | solution.py:394
  11.4 0.0 copy-done.2
  11.5 0.0 copy-done.5
  11.5 0.0 copy-done.6
  11.5 0.7 %parents.1 = (f32[8,8,128]{2,1,0:T(8,128)S(1)}, f32[8,40,128]{2,1,0:T(8,128)S(1)}) custom-call(f32[3,3,64,128]{3,2,1,0:T(8,128)S(1)} %bitcast.3, f32[3,3,32,64]{3,2,1,0:T(8,128)S(1)} %bitcast.7, f32[3,3,3,64]{3,2,1,0:T(4,128)S(1)} %bitcast.8), custom_call_target="tpu_custom_call" | custom-call | bytes 160000 | tf_op jit(solution)/shard_map/parents/pallas_call | solution.py:394
  12.2 0.0 collective-permute-done.2.rest_3_
  12.2 4.7 %collective-permute-done.3.rest_4_ = f32[6,32,128]{2,1,0:T(8,128)S(1)} collective-permute-done((f32[6,32,128]{2,1,0:T(8,128)S(1)}, f32[6,32,128]{2,1,0:T(8,128)S(1)}, u32[]{:S(2)}, u32[]{:S(2)}) %collective-permute-start.3) | collective-permute-done | bytes 98336 | tf_op jit(solution)/shard_map/ppermute | solution.py:430
  16.8 0.0 copy-done.4
  16.8 1.8 %inner1.1 = (f32[64,32,128]{2,1,0:T(8,128)S(1)}, f32[64,32,128]{2,1,0:T(8,128)S(1)}, f32[64,32,128]{2,1,0:T(8,128)S(1)}, f32[64,16,128]{2,1,0:T(8,128)S(1)}) custom-call(f32[64,32,128]{2,1,0:T(8,128)S(1)} %copy-done, f32[64,32,128]{2,1,0:T(8,128)S(1)} %copy-done.3, f32[64,16,128]{2,1,0:T(8,128)S(1)} %get-tuple-element.38.ex, ...), custom_call_target="tpu_custom_call" | custom-call | bytes 960000 | tf_op jit(solution)/shard_map/inner1/pallas_call | solution.py:394
  18.7 0.0 collective-permute-done.x1
  18.7 0.0 collective-permute-done.1.x2
  18.7 1.0 %outer1.1 = (f32[64,32,128]{2,1,0:T(8,128)S(1)}, f32[64,48,128]{2,1,0:T(8,128)S(1)}, f32[384,128]{1,0:T(8,128)S(1)}, f32[384,128]{1,0:T(8,128)S(1)}) custom-call(f32[576,128]{1,0:T(8,128)S(1)} %collective-permute-done.x1, f32[576,128]{1,0:T(8,128)S(1)} %collective-permute-done.1.x2, ...), custom_call_target="tpu_custom_call", output_to_operand_aliasing={{0}: (7, {}), {1}: (8, {})} | custom-call | bytes 160000 | tf_op jit(solution)/shard_map/outer1/pallas_call | solution.py:394
  19.7 0.1 collective-permute-start.4
  19.8 1.2 %collective-permute-start.5 = (f32[384,128]{1,0:T(8,128)S(1)}, f32[384,128]{1,0:T(8,128)S(1)}, u32[]{:S(2)}, u32[]{:S(2)}) collective-permute-start(f32[384,128]{1,0:T(8,128)S(1)} %get-tuple-element.47), channel_id=1, source_target_pairs={{0,112},{16,32},{32,16},{48,64},{64,48},{80,96},{96,80},{112,0},{1... | collective-permute-start | bytes 589832 | tf_op jit(solution)/shard_map/ppermute | solution.py:462
  21.0 0.3 y_pack.1
  21.3 2.4 %collective-permute-start.6 = (f32[4,32,128]{2,1,0:T(8,128)S(1)}, f32[4,32,128]{2,1,0:T(8,128)S(1)}, u32[]{:S(2)}, u32[]{:S(2)}) collective-permute-start(f32[4,32,128]{2,1,0:T(8,128)S(1)} %get-tuple-element.53), channel_id=1, source_target_pairs={{0,1},{1,0},{2,3},{3,2},{4,5},{5,4},{6,7},{7,6},{8,9},{9,8},{10,11... | collective-permute-start | bytes 196616 | tf_op jit(solution)/shard_map/ppermute | solution.py:467
  23.7 0.6 %collective-permute-start.7 = (f32[4,32,128]{2,1,0:T(8,128)S(1)}, f32[4,32,128]{2,1,0:T(8,128)S(1)}, u32[]{:S(2)}, u32[]{:S(2)}) collective-permute-start(f32[4,32,128]{2,1,0:T(8,128)S(1)} %get-tuple-element.54), channel_id=1, source_target_pairs={{0,15},{1,2},{2,1},{3,4},{4,3},{5,6},{6,5},{7,8},{8,7},{9,10},{10,... | collective-permute-start | bytes 196616 | tf_op jit(solution)/shard_map/ppermute | solution.py:468
  24.4 0.6 %across2.1 = (f32[64,48,128]{2,1,0:T(8,128)S(1)}, f32[64,16,128]{2,1,0:T(8,128)S(1)}) custom-call(f32[64,32,128]{2,1,0:T(8,128)S(1)} %get-tuple-element.48.p, f32[64,48,128]{2,1,0:T(8,128)S(1)} %get-tuple-element.49.u), custom_call_target="tpu_custom_call" | custom-call | bytes 160000 | tf_op jit(solution)/shard_map/across2/pallas_call | solution.py:394
  24.9 0.0 collective-permute-done.6.rest_4_
  25.0 4.6 %collective-permute-done.7.rest_5_ = f32[4,32,128]{2,1,0:T(8,128)S(1)} collective-permute-done((f32[4,32,128]{2,1,0:T(8,128)S(1)}, f32[4,32,128]{2,1,0:T(8,128)S(1)}, u32[]{:S(2)}, u32[]{:S(2)}) %collective-permute-start.7) | collective-permute-done | bytes 65568 | tf_op jit(solution)/shard_map/ppermute | solution.py:468
  29.6 1.8 %inner2.1 = (f32[64,32,128]{2,1,0:T(8,128)S(1)}, f32[64,32,128]{2,1,0:T(8,128)S(1)}, f32[64,16,128]{2,1,0:T(8,128)S(1)}) custom-call(f32[64,32,128]{2,1,0:T(8,128)S(1)} %get-tuple-element.48.p, f32[64,32,128]{2,1,0:T(8,128)S(1)} %get-tuple-element.50.v, f32[64,16,128]{2,1,0:T(8,128)S(1)} %get-tuple-element.51.ex, ...), custom_call_target="tpu_custom_call" | custom-call | bytes 960000 | tf_op jit(solution)/shard_map/inner2/pallas_call | solution.py:394
  31.4 0.0 collective-permute-done.4.x1
  31.4 0.0 collective-permute-done.5.x2
  31.4 0.9 %outer2.1 = (f32[64,32,128]{2,1,0:T(8,128)S(1)}, f32[64,48,128]{2,1,0:T(8,128)S(1)}, f32[384,128]{1,0:T(8,128)S(1)}) custom-call(f32[384,128]{1,0:T(8,128)S(1)} %collective-permute-done.4.x1, f32[384,128]{1,0:T(8,128)S(1)} %collective-permute-done.5.x2, f32[64,32,128]{2,1,0:T(8,128)S(1)} %get-tuple-element.48.p, ...), custom_call_target="tpu_custom_call", output_to_operand_aliasing={{0}: (7, {}), {1}: (8, {})} | custom-call | bytes 160000 | tf_op jit(solution)/shard_map/outer2/pallas_call | solution.py:394
  32.3 0.1 collective-permute-start.8
  32.4 0.3 corner_pack.1.after
  32.7 0.0 copy-start.8
  32.7 0.8 %north_pack.1 = f32[8,32,128]{2,1,0:T(8,128)S(1)} custom-call(f32[64,48,128]{2,1,0:T(8,128)S(1)} %get-tuple-element.59.u, f32[64,32,128]{2,1,0:T(8,128)S(1)} %get-tuple-element.58.tail_0_.v, f32[64,32,128]{2,1,0:T(8,128)S(1)} %get-tuple-element.60.p, f32[8,40,128]{2,1,0:T(8,128)S(1)} %get-tuple-element.42.rest_6_.pn, f32[8,8,128]{2,1,0:T(8,128)S(1)} %corner_pack.1.after), custom_call_target="tpu_custom_call" | custom-call | bytes 160000 | tf_op jit(solution)/shard_map/north_pack/pallas_call | solution.py:394
  33.6 0.3 collective-permute-start.9
  33.8 0.1 collective-permute-start.10
  33.9 0.0 copy-done.8
  33.9 1.7 %turn.1 = (f32[64,32,128]{2,1,0:T(8,128)S(1)}, f32[64,32,128]{2,1,0:T(8,128)S(1)}, f32[64,32,128]{2,1,0:T(8,128)S(1)}) custom-call(s32[2]{0:T(128)S(1)} %copy-done.8, f32[64,48,128]{2,1,0:T(8,128)S(1)} %get-tuple-element.59.u, f32[64,32,128]{2,1,0:T(8,128)S(1)} %get-tuple-element.58.tail_0_.v, f32[64,32,128]{2,1,0:T(8,128)S(1)} %get-tuple-element.60.p, ...), custom_call_target="tpu_custom_call" | custom-call | bytes 160000 | tf_op jit(solution)/shard_map/turn/pallas_call | solution.py:394
  35.6 9.0 %collective-permute-done.10.corner = f32[8,8,128]{2,1,0:T(8,128)S(1)} collective-permute-done((f32[8,8,128]{2,1,0:T(8,128)S(1)}, f32[8,8,128]{2,1,0:T(8,128)S(1)}, u32[]{:S(2)}, u32[]{:S(2)}) %collective-permute-start.10) | collective-permute-done | bytes 32800 | tf_op jit(solution)/shard_map/ppermute | solution.py:495
  44.6 0.0 collective-permute-done.9.north
  44.6 0.0 collective-permute-done.8.east
  44.6 2.7 %move.1 = (f32[64,32,128]{2,1,0:T(8,128)}, f32[64,32,128]{2,1,0:T(8,128)}, f32[64,32,128]{2,1,0:T(8,128)}) custom-call(s32[2]{0:T(128)S(1)} %copy-done.8, f32[64,32,128]{2,1,0:T(8,128)S(1)} %get-tuple-element.61.ru, f32[64,32,128]{2,1,0:T(8,128)S(1)} %get-tuple-element.62.rv, f32[64,32,128]{2,1,0:T(8,128)S(1)} %get-tuple-element.63.rp, ...), custom_call_target="tpu_custom_call" | custom-call | bytes 160000 | tf_op jit(solution)/shard_map/move/pallas_call | solution.py:394
Async XLA Ops:
  0.6 7.0 %copy-start = (f32[64,32,128]{2,1,0:T(8,128)S(1)}, f32[64,32,128]{2,1,0:T(8,128)}, u32[]{:S(2)}) copy-start(f32[64,32,128]{2,1,0:T(8,128)} %p.9) | copy-start | bytes 3145732
  0.6 6.9 %copy-start.3 = (f32[64,32,128]{2,1,0:T(8,128)S(1)}, f32[64,32,128]{2,1,0:T(8,128)}, u32[]{:S(2)}) copy-start(f32[64,32,128]{2,1,0:T(8,128)} %v.3) | copy-start | bytes 3145732
  2.9 7.3 %copy-start.1 = (f32[64,32,128]{2,1,0:T(8,128)S(1)}, f32[64,32,128]{2,1,0:T(8,128)}, u32[]{:S(2)}) copy-start(f32[64,32,128]{2,1,0:T(8,128)} %u.5) | copy-start | bytes 3145732
  3.0 15.7 %collective-permute-start = (f32[576,128]{1,0:T(8,128)}, f32[576,128]{1,0:T(8,128)S(1)}, u32[]{:S(2)}, u32[]{:S(2)}) collective-permute-start(f32[576,128]{1,0:T(8,128)} %get-tuple-element.34), channel_id=1, source_target_pairs={{0,16},{16,0},{32,48},{48,32},{64,80},{80,64},{96,112},{112,96},{1... | collective-permute-start | bytes 884744 | tf_op jit(solution)/shard_map/ppermute | solution.py:425
  3.5 15.2 %collective-permute-start.1 = (f32[576,128]{1,0:T(8,128)}, f32[576,128]{1,0:T(8,128)S(1)}, u32[]{:S(2)}, u32[]{:S(2)}) collective-permute-start(f32[576,128]{1,0:T(8,128)} %get-tuple-element.35), channel_id=1, source_target_pairs={{0,112},{16,32},{32,16},{48,64},{64,48},{80,96},{96,80},{112,0},{1... | collective-permute-start | bytes 884744 | tf_op jit(solution)/shard_map/ppermute | solution.py:424
  8.3 2.6 %copy-start.7 = (f32[32,128]{1,0:T(8,128)S(1)}, f32[32,128]{1,0:T(8,128)}, u32[]{:S(2)}) copy-start(f32[32,128]{1,0:T(8,128)} %s_ref.1) | copy-start | bytes 49156
  8.3 3.2 %copy-start.2 = (f32[3,64,3,128]{3,1,2,0:T(8,128)S(1)}, f32[3,64,3,128]{3,1,2,0:T(8,128)}, u32[]{:S(2)}) copy-start(f32[3,64,3,128]{3,1,2,0:T(8,128)} %param.13) | copy-start | bytes 884740
  8.3 3.2 %copy-start.5 = (f32[3,64,32,3]{1,2,3,0:T(8,128)S(1)}, f32[3,64,32,3]{1,2,3,0:T(8,128)}, u32[]{:S(2)}) copy-start(f32[3,64,32,3]{1,2,3,0:T(8,128)} %param.14) | copy-start | bytes 221188
  8.3 3.2 %copy-start.6 = (f32[3,64,3,3]{1,3,2,0:T(4,128)S(1)}, f32[3,64,3,3]{1,3,2,0:T(4,128)}, u32[]{:S(2)}) copy-start(f32[3,64,3,3]{1,3,2,0:T(4,128)} %param.15) | copy-start | bytes 20740
  8.3 8.5 %copy-start.4 = (bf16[256,256]{1,0:T(8,128)(2,1)S(1)}, bf16[256,256]{1,0:T(8,128)(2,1)}, u32[]{:S(2)}) copy-start(bf16[256,256]{1,0:T(8,128)(2,1)} %constant.2.clone.rest_2_.rest_3_) | copy-start | bytes 393220
  8.3 3.8 %collective-permute-start.2 = (f32[6,32,128]{2,1,0:T(8,128)S(1)}, f32[6,32,128]{2,1,0:T(8,128)S(1)}, u32[]{:S(2)}, u32[]{:S(2)}) collective-permute-start(f32[6,32,128]{2,1,0:T(8,128)S(1)} %get-tuple-element.39), channel_id=1, source_target_pairs={{0,1},{1,0},{2,3},{3,2},{4,5},{5,4},{6,7},{7,6},{8,9},{9,8},{10,11... | collective-permute-start | bytes 294920 | tf_op jit(solution)/shard_map/ppermute | solution.py:429
  9.6 7.2 %collective-permute-start.3 = (f32[6,32,128]{2,1,0:T(8,128)S(1)}, f32[6,32,128]{2,1,0:T(8,128)S(1)}, u32[]{:S(2)}, u32[]{:S(2)}) collective-permute-start(f32[6,32,128]{2,1,0:T(8,128)S(1)} %get-tuple-element.40), channel_id=1, source_target_pairs={{0,15},{1,2},{2,1},{3,4},{4,3},{5,6},{6,5},{7,8},{8,7},{9,10},{10,... | collective-permute-start | bytes 294920 | tf_op jit(solution)/shard_map/ppermute | solution.py:430
  19.7 11.7 %collective-permute-start.4 = (f32[384,128]{1,0:T(8,128)S(1)}, f32[384,128]{1,0:T(8,128)S(1)}, u32[]{:S(2)}, u32[]{:S(2)}) collective-permute-start(f32[384,128]{1,0:T(8,128)S(1)} %get-tuple-element.46), channel_id=1, source_target_pairs={{0,16},{16,0},{32,48},{48,32},{64,80},{80,64},{96,112},{112,96},{1... | collective-permute-start | bytes 589832 | tf_op jit(solution)/shard_map/ppermute | solution.py:463
  19.8 11.7 %collective-permute-start.5 = (f32[384,128]{1,0:T(8,128)S(1)}, f32[384,128]{1,0:T(8,128)S(1)}, u32[]{:S(2)}, u32[]{:S(2)}) collective-permute-start(f32[384,128]{1,0:T(8,128)S(1)} %get-tuple-element.47), channel_id=1, source_target_pairs={{0,112},{16,32},{32,16},{48,64},{64,48},{80,96},{96,80},{112,0},{1... | collective-permute-start | bytes 589832 | tf_op jit(solution)/shard_map/ppermute | solution.py:462
  21.3 3.6 %collective-permute-start.6 = (f32[4,32,128]{2,1,0:T(8,128)S(1)}, f32[4,32,128]{2,1,0:T(8,128)S(1)}, u32[]{:S(2)}, u32[]{:S(2)}) collective-permute-start(f32[4,32,128]{2,1,0:T(8,128)S(1)} %get-tuple-element.53), channel_id=1, source_target_pairs={{0,1},{1,0},{2,3},{3,2},{4,5},{5,4},{6,7},{7,6},{8,9},{9,8},{10,11... | collective-permute-start | bytes 196616 | tf_op jit(solution)/shard_map/ppermute | solution.py:467
  23.7 5.9 %collective-permute-start.7 = (f32[4,32,128]{2,1,0:T(8,128)S(1)}, f32[4,32,128]{2,1,0:T(8,128)S(1)}, u32[]{:S(2)}, u32[]{:S(2)}) collective-permute-start(f32[4,32,128]{2,1,0:T(8,128)S(1)} %get-tuple-element.54), channel_id=1, source_target_pairs={{0,15},{1,2},{2,1},{3,4},{4,3},{5,6},{6,5},{7,8},{8,7},{9,10},{10,... | collective-permute-start | bytes 196616 | tf_op jit(solution)/shard_map/ppermute | solution.py:468
  32.3 12.3 %collective-permute-start.8 = (f32[384,128]{1,0:T(8,128)S(1)}, f32[384,128]{1,0:T(8,128)S(1)}, u32[]{:S(2)}, u32[]{:S(2)}) collective-permute-start(f32[384,128]{1,0:T(8,128)S(1)} %get-tuple-element.64), channel_id=1, source_target_pairs={{0,112},{16,0},{32,16},{48,32},{64,48},{80,64},{96,80},{112,96},{1... | collective-permute-start | bytes 589832 | tf_op jit(solution)/shard_map/ppermute | solution.py:491
  32.7 1.2 %copy-start.8 = (s32[2]{0:T(128)S(1)}, s32[2]{0:T(128)}, u32[]{:S(2)}) copy-start(s32[2]{0:T(128)} %offsets.3) | copy-start | bytes 28
  33.6 11.1 %collective-permute-start.9 = (f32[8,32,128]{2,1,0:T(8,128)S(1)}, f32[8,32,128]{2,1,0:T(8,128)S(1)}, u32[]{:S(2)}, u32[]{:S(2)}) collective-permute-start(f32[8,32,128]{2,1,0:T(8,128)S(1)} %north_pack.1), channel_id=1, source_target_pairs={{0,15},{1,0},{2,1},{3,2},{4,3},{5,4},{6,5},{7,6},{8,7},{9,8},{10,9... | collective-permute-start | bytes 393224 | tf_op jit(solution)/shard_map/ppermute | solution.py:499
  33.8 10.8 %collective-permute-start.10 = (f32[8,8,128]{2,1,0:T(8,128)S(1)}, f32[8,8,128]{2,1,0:T(8,128)S(1)}, u32[]{:S(2)}, u32[]{:S(2)}) collective-permute-start(f32[8,8,128]{2,1,0:T(8,128)S(1)} %corner_pack.1.after), channel_id=1, source_target_pairs={{0,127},{1,112},{2,113},{3,114},{4,115},{5,116},{6,117},{7,118},{8... | collective-permute-start | bytes 98312 | tf_op jit(solution)/shard_map/ppermute | solution.py:495

commit v3 on v2

--- a/solution.py
+++ b/solution.py
@@ -41,9 +41,8 @@
 def dy(ext, mat):
     hi = ext.astype(BF16)
     lo = (ext - hi.astype(F32)).astype(BF16)
-    return jnp.dot(hi, mat, preferred_element_type=F32) + jnp.dot(
-        lo, mat, preferred_element_type=F32
-    )
+    both = jnp.dot(jnp.concatenate([hi, lo], axis=0), mat, preferred_element_type=F32)
+    return both[: ext.shape[0]] + both[ext.shape[0] :]
 
 
 def pack_edges(rows, step, lanes):
@@ -325,8 +324,8 @@
 
 
 def turn_kernel(offsets, u, v, p, pe, ru, rv, rp, tu, tv, tp):
-    o0 = offsets[0]
-    shift = lax.rem(128 - offsets[1], 128)
+    o0 = offsets[0, 0]
+    shift = lax.rem(128 - offsets[0, 1], 128)
     for l in range(64):
         tu[40 * l : 40 * l + 40, :] = pltpu.roll(u[l, 8:48, :], shift, 1)
         tv[40 * l : 40 * l + 32, :] = pltpu.roll(v[l], shift, 1)
@@ -345,7 +344,7 @@
 
 def move_kernel(offsets, ru, rv, rp, east, north, corner, ou, ov, op, bu, bv, bp, ns, columns, sems):
     lanes = lane_index()
-    o0, o1 = offsets[0], offsets[1]
+    o0, o1 = offsets[0, 0], offsets[0, 1]
     own_lane = lanes < 128 - o1
     own_row = lax.broadcasted_iota(jnp.int32, (8, 128), 0) < 8 - o0
     shift = lax.rem(128 - o1, 128)
@@ -419,7 +418,7 @@
         buffers(*[(64, 8, 128)] * 4) + [dma((4,))],
         name="x_edges",
         specs={0: HBM, 1: HBM},
-        vmem=60,
+        vmem=53,
     )
     x2 = lax.ppermute(second, "gx", x_out)
     x1 = lax.ppermute(first, "gx", x_in)
@@ -497,13 +496,13 @@
         north_pack_kernel, sds(8, 32, 128), (u2, v2, p2, pn_strip, corner), name="north_pack"
     )
     north = lax.ppermute(north, "gy", down_y)
+    offsets = jnp.pad(offsets.reshape(1, 2), ((0, 7), (0, 126)))
     ru, rv, rp = call(
         turn_kernel,
         (field, field, field),
         (offsets, u2, v2, p2, pe),
         buffers(*[(64 * 40, 128)] * 3),
         name="turn",
-        specs={0: SMEM},
     )
     return call(
         move_kernel,
@@ -512,7 +511,6 @@
         buffers(*[(64, 32, 128)] * 3, (8, 40, 128), (392, 128))
         + [dma((24,))],
         name="move",
-        specs={0: SMEM},
         outs=ANY,
     )
 

time: 47.9 us -> 45.9 us (0.958)
  Pallas kernels: 16.7 us -> 14.6 us
    pallas_call x15, Pallas kernels: 16.7 us -> 14.6 us  [call(): pl.pallas_call(body, out_shape=out_shape, in_specs=[specs.get(k, VMEM) fo...]
  transfers between devices with their start and end apart: 11 -> 11, of which waited for: 3 -> 3; matrix products, arithmetic and copies ran while one was open for 0% -> 0% of each run, Pallas kernels for 21% -> 20%
where the time goes in v3:
time: 45.9 us; the launch traced here: 45.4 us
  waiting for transfers between devices  18.8 us (41%)
  Pallas kernels  14.6 us (32%)
  starting transfers between devices  11.1 us (24%)
  between operations  0.92 us (2%)
    pallas_call x15, Pallas kernels, call(): pl.pallas_call(body, out_shape=out_shape, in_specs=[specs.get(k, VMEM) fo...  14.6 us
    ppermute x1, waiting for transfers between devices, on_device(): from_corner = lax.ppermute(corner, ('gx', 'gy'), down)  9.46 us
    ppermute x2, waiting for transfers between devices, on_device(): y2 = lax.ppermute(second, 'gy', y_out)  9.3 us
    ppermute x2, starting transfers between devices, on_device(): x2 = lax.ppermute(second, 'gx', x_out)  5.32 us
    ppermute x2, starting transfers between devices, on_device(): y1 = lax.ppermute(first, 'gy', y_in)  3.68 us
    ppermute x2, starting transfers between devices, on_device(): y2 = lax.ppermute(second, 'gy', y_out)  1.26 us
  transfers between devices with their start and end apart: 11, of which 3 were waited for; matrix products, arithmetic and copies ran while one was open for 0% of the time, Pallas kernels for 20%

profile of v3, /device:TPU:31, one launch (start us, length us, event | category | flops | bytes accessed | tf_op | source)
XLA Modules:
  0.0 45.4 jit_solution(6196778529749729215)
XLA Ops:
  0.6 0.0 copy-start
  0.6 0.0 copy-start.3
  0.7 1.5 %x_edges.1 = (f32[576,128]{1,0:T(8,128)S(1)}, f32[576,128]{1,0:T(8,128)S(1)}) custom-call(f32[64,32,128]{2,1,0:T(8,128)} %p.9, f32[64,32,128]{2,1,0:T(8,128)} %u.5), custom_call_target="tpu_custom_call" | custom-call | bytes 160000 | tf_op jit(solution)/shard_map/x_edges/pallas_call | solution.py:393
  2.1 0.0 copy-start.1
  2.1 0.5 %collective-permute-start = (f32[576,128]{1,0:T(8,128)S(1)}, f32[576,128]{1,0:T(8,128)S(1)}, u32[]{:S(2)}, u32[]{:S(2)}) collective-permute-start(f32[576,128]{1,0:T(8,128)S(1)} %get-tuple-element.34), channel_id=1, source_target_pairs={{0,16},{16,0},{32,48},{48,32},{64,80},{80,64},{96,112},{112,96},{1... | collective-permute-start | bytes 884744 | tf_op jit(solution)/shard_map/ppermute | solution.py:424
  2.7 4.1 %collective-permute-start.1 = (f32[576,128]{1,0:T(8,128)S(1)}, f32[576,128]{1,0:T(8,128)S(1)}, u32[]{:S(2)}, u32[]{:S(2)}) collective-permute-start(f32[576,128]{1,0:T(8,128)S(1)} %get-tuple-element.35), channel_id=1, source_target_pairs={{0,112},{16,32},{32,16},{48,64},{64,48},{80,96},{96,80},{112,0},{1... | collective-permute-start | bytes 884744 | tf_op jit(solution)/shard_map/ppermute | solution.py:423
  6.8 0.0 copy-done
  6.8 0.0 copy-done.3
  6.8 0.7 %y_edges.1 = (f32[6,32,128]{2,1,0:T(8,128)S(1)}, f32[6,32,128]{2,1,0:T(8,128)S(1)}) custom-call(f32[64,32,128]{2,1,0:T(8,128)S(1)} %copy-done, f32[64,32,128]{2,1,0:T(8,128)S(1)} %copy-done.3), custom_call_target="tpu_custom_call" | custom-call | bytes 160000 | tf_op jit(solution)/shard_map/y_edges/pallas_call | solution.py:393
  7.5 0.0 copy-start.7
  7.5 0.0 copy-start.2
  7.5 0.0 copy-start.5
  7.5 0.0 copy-start.6
  7.5 0.0 copy-start.4
  7.5 1.3 %collective-permute-start.2 = (f32[6,32,128]{2,1,0:T(8,128)S(1)}, f32[6,32,128]{2,1,0:T(8,128)S(1)}, u32[]{:S(2)}, u32[]{:S(2)}) collective-permute-start(f32[6,32,128]{2,1,0:T(8,128)S(1)} %get-tuple-element.39), channel_id=1, source_target_pairs={{0,1},{1,0},{2,3},{3,2},{4,5},{5,4},{6,7},{7,6},{8,9},{9,8},{10,11... | collective-permute-start | bytes 294920 | tf_op jit(solution)/shard_map/ppermute | solution.py:428
  8.8 0.6 %collective-permute-start.3 = (f32[6,32,128]{2,1,0:T(8,128)S(1)}, f32[6,32,128]{2,1,0:T(8,128)S(1)}, u32[]{:S(2)}, u32[]{:S(2)}) collective-permute-start(f32[6,32,128]{2,1,0:T(8,128)S(1)} %get-tuple-element.40), channel_id=1, source_target_pairs={{0,15},{1,2},{2,1},{3,4},{4,3},{5,6},{6,5},{7,8},{8,7},{9,10},{10,... | collective-permute-start | bytes 294920 | tf_op jit(solution)/shard_map/ppermute | solution.py:429
  9.5 0.0 copy-done.1
  9.5 0.6 %across1.1 = (f32[64,48,128]{2,1,0:T(8,128)S(1)}, f32[64,16,128]{2,1,0:T(8,128)S(1)}) custom-call(f32[64,32,128]{2,1,0:T(8,128)S(1)} %copy-done, f32[64,32,128]{2,1,0:T(8,128)S(1)} %copy-done.1), custom_call_target="tpu_custom_call" | custom-call | bytes 160000 | tf_op jit(solution)/shard_map/across1/pallas_call | solution.py:393
  10.1 0.0 copy-done.7
  10.1 0.6 %coefficients.1 = (f32[64,32,128]{2,1,0:T(8,128)S(1)}, f32[64,32,128]{2,1,0:T(8,128)S(1)}) custom-call(f32[32,128]{1,0:T(8,128)S(1)} %copy-done.7), custom_call_target="tpu_custom_call" | custom-call | bytes 160000 | tf_op jit(solution)/shard_map/coefficients/pallas_call | solution.py:393
  10.6 0.0 copy-done.2
  10.6 0.0 copy-done.5
  10.7 0.0 copy-done.6
  10.7 0.7 %parents.1 = (f32[8,8,128]{2,1,0:T(8,128)S(1)}, f32[8,40,128]{2,1,0:T(8,128)S(1)}) custom-call(f32[3,3,64,128]{3,2,1,0:T(8,128)S(1)} %bitcast.4, f32[3,3,32,64]{3,2,1,0:T(8,128)S(1)} %bitcast.8, f32[3,3,3,64]{3,2,1,0:T(4,128)S(1)} %bitcast.9), custom_call_target="tpu_custom_call" | custom-call | bytes 160000 | tf_op jit(solution)/shard_map/parents/pallas_call | solution.py:393
  11.4 0.0 collective-permute-done.2.rest_3_
  11.4 4.7 %collective-permute-done.3.rest_4_ = f32[6,32,128]{2,1,0:T(8,128)S(1)} collective-permute-done((f32[6,32,128]{2,1,0:T(8,128)S(1)}, f32[6,32,128]{2,1,0:T(8,128)S(1)}, u32[]{:S(2)}, u32[]{:S(2)}) %collective-permute-start.3) | collective-permute-done | bytes 98336 | tf_op jit(solution)/shard_map/ppermute | solution.py:429
  16.0 0.0 copy-done.4
  16.0 1.6 %inner1.1 = (f32[64,32,128]{2,1,0:T(8,128)S(1)}, f32[64,32,128]{2,1,0:T(8,128)S(1)}, f32[64,32,128]{2,1,0:T(8,128)S(1)}, f32[64,16,128]{2,1,0:T(8,128)S(1)}) custom-call(f32[64,32,128]{2,1,0:T(8,128)S(1)} %copy-done, f32[64,32,128]{2,1,0:T(8,128)S(1)} %copy-done.3, f32[64,16,128]{2,1,0:T(8,128)S(1)} %get-tuple-element.38.ex, ...), custom_call_target="tpu_custom_call" | custom-call | bytes 960000 | tf_op jit(solution)/shard_map/inner1/pallas_call | solution.py:393
  17.7 0.0 collective-permute-done.x1
  17.7 0.0 collective-permute-done.1.x2
  17.7 1.0 %outer1.1 = (f32[64,32,128]{2,1,0:T(8,128)S(1)}, f32[64,48,128]{2,1,0:T(8,128)S(1)}, f32[384,128]{1,0:T(8,128)S(1)}, f32[384,128]{1,0:T(8,128)S(1)}) custom-call(f32[576,128]{1,0:T(8,128)S(1)} %collective-permute-done.x1, f32[576,128]{1,0:T(8,128)S(1)} %collective-permute-done.1.x2, ...), custom_call_target="tpu_custom_call", output_to_operand_aliasing={{0}: (7, {}), {1}: (8, {})} | custom-call | bytes 160000 | tf_op jit(solution)/shard_map/outer1/pallas_call | solution.py:393
  18.7 0.1 collective-permute-start.4
  18.8 1.2 %collective-permute-start.5 = (f32[384,128]{1,0:T(8,128)S(1)}, f32[384,128]{1,0:T(8,128)S(1)}, u32[]{:S(2)}, u32[]{:S(2)}) collective-permute-start(f32[384,128]{1,0:T(8,128)S(1)} %get-tuple-element.47), channel_id=1, source_target_pairs={{0,112},{16,32},{32,16},{48,64},{64,48},{80,96},{96,80},{112,0},{1... | collective-permute-start | bytes 589832 | tf_op jit(solution)/shard_map/ppermute | solution.py:461
  20.0 0.3 y_pack.1
  20.3 2.4 %collective-permute-start.6 = (f32[4,32,128]{2,1,0:T(8,128)S(1)}, f32[4,32,128]{2,1,0:T(8,128)S(1)}, u32[]{:S(2)}, u32[]{:S(2)}) collective-permute-start(f32[4,32,128]{2,1,0:T(8,128)S(1)} %get-tuple-element.53), channel_id=1, source_target_pairs={{0,1},{1,0},{2,3},{3,2},{4,5},{5,4},{6,7},{7,6},{8,9},{9,8},{10,11... | collective-permute-start | bytes 196616 | tf_op jit(solution)/shard_map/ppermute | solution.py:466
  22.7 0.6 %collective-permute-start.7 = (f32[4,32,128]{2,1,0:T(8,128)S(1)}, f32[4,32,128]{2,1,0:T(8,128)S(1)}, u32[]{:S(2)}, u32[]{:S(2)}) collective-permute-start(f32[4,32,128]{2,1,0:T(8,128)S(1)} %get-tuple-element.54), channel_id=1, source_target_pairs={{0,15},{1,2},{2,1},{3,4},{4,3},{5,6},{6,5},{7,8},{8,7},{9,10},{10,... | collective-permute-start | bytes 196616 | tf_op jit(solution)/shard_map/ppermute | solution.py:467
  23.3 0.6 %across2.1 = (f32[64,48,128]{2,1,0:T(8,128)S(1)}, f32[64,16,128]{2,1,0:T(8,128)S(1)}) custom-call(f32[64,32,128]{2,1,0:T(8,128)S(1)} %get-tuple-element.48.p, f32[64,48,128]{2,1,0:T(8,128)S(1)} %get-tuple-element.49.u), custom_call_target="tpu_custom_call" | custom-call | bytes 160000 | tf_op jit(solution)/shard_map/across2/pallas_call | solution.py:393
  23.9 0.0 collective-permute-done.6.rest_4_
  23.9 4.6 %collective-permute-done.7.rest_5_ = f32[4,32,128]{2,1,0:T(8,128)S(1)} collective-permute-done((f32[4,32,128]{2,1,0:T(8,128)S(1)}, f32[4,32,128]{2,1,0:T(8,128)S(1)}, u32[]{:S(2)}, u32[]{:S(2)}) %collective-permute-start.7) | collective-permute-done | bytes 65568 | tf_op jit(solution)/shard_map/ppermute | solution.py:467
  28.6 1.6 %inner2.1 = (f32[64,32,128]{2,1,0:T(8,128)S(1)}, f32[64,32,128]{2,1,0:T(8,128)S(1)}, f32[64,16,128]{2,1,0:T(8,128)S(1)}) custom-call(f32[64,32,128]{2,1,0:T(8,128)S(1)} %get-tuple-element.48.p, f32[64,32,128]{2,1,0:T(8,128)S(1)} %get-tuple-element.50.v, f32[64,16,128]{2,1,0:T(8,128)S(1)} %get-tuple-element.51.ex, ...), custom_call_target="tpu_custom_call" | custom-call | bytes 960000 | tf_op jit(solution)/shard_map/inner2/pallas_call | solution.py:393
  30.2 0.0 collective-permute-done.4.x1
  30.2 0.0 collective-permute-done.5.x2
  30.2 0.9 %outer2.1 = (f32[64,32,128]{2,1,0:T(8,128)S(1)}, f32[64,48,128]{2,1,0:T(8,128)S(1)}, f32[384,128]{1,0:T(8,128)S(1)}) custom-call(f32[384,128]{1,0:T(8,128)S(1)} %collective-permute-done.4.x1, f32[384,128]{1,0:T(8,128)S(1)} %collective-permute-done.5.x2, f32[64,32,128]{2,1,0:T(8,128)S(1)} %get-tuple-element.48.p, ...), custom_call_target="tpu_custom_call", output_to_operand_aliasing={{0}: (7, {}), {1}: (8, {})} | custom-call | bytes 160000 | tf_op jit(solution)/shard_map/outer2/pallas_call | solution.py:393
  31.1 0.1 collective-permute-start.8
  31.2 0.3 corner_pack.1.after
  31.5 0.0 copy-start.8
  31.5 0.8 %north_pack.1 = f32[8,32,128]{2,1,0:T(8,128)S(1)} custom-call(f32[64,48,128]{2,1,0:T(8,128)S(1)} %get-tuple-element.59.u, f32[64,32,128]{2,1,0:T(8,128)S(1)} %get-tuple-element.58.tail_0_.v, f32[64,32,128]{2,1,0:T(8,128)S(1)} %get-tuple-element.60.p, f32[8,40,128]{2,1,0:T(8,128)S(1)} %get-tuple-element.42.rest_6_.pn, f32[8,8,128]{2,1,0:T(8,128)S(1)} %corner_pack.1.after), custom_call_target="tpu_custom_call" | custom-call | bytes 160000 | tf_op jit(solution)/shard_map/north_pack/pallas_call | solution.py:393
  32.3 0.1 collective-permute-start.9
  32.4 0.1 collective-permute-start.10
  32.5 0.0 copy-done.8
  32.5 1.2 %turn.1 = (f32[64,32,128]{2,1,0:T(8,128)S(1)}, f32[64,32,128]{2,1,0:T(8,128)S(1)}, f32[64,32,128]{2,1,0:T(8,128)S(1)}) custom-call(s32[8,128]{1,0:T(8,128)S(1)} %pad.4.offsets, f32[64,48,128]{2,1,0:T(8,128)S(1)} %get-tuple-element.59.u, f32[64,32,128]{2,1,0:T(8,128)S(1)} %get-tuple-element.58.tail_0_.v, f32[64,32,128]{2,1,0:T(8,128)S(1)} %get-tuple-element.60.p, ...), custom_call_target="tpu_custom_call" | custom-call | bytes 160000 | tf_op jit(solution)/shard_map/turn/pallas_call | solution.py:393
  33.8 9.5 %collective-permute-done.10.corner = f32[8,8,128]{2,1,0:T(8,128)S(1)} collective-permute-done((f32[8,8,128]{2,1,0:T(8,128)S(1)}, f32[8,8,128]{2,1,0:T(8,128)S(1)}, u32[]{:S(2)}, u32[]{:S(2)}) %collective-permute-start.10) | collective-permute-done | bytes 32800 | tf_op jit(solution)/shard_map/ppermute | solution.py:494
  43.2 0.0 collective-permute-done.9.north
  43.3 0.0 collective-permute-done.8.east
  43.3 2.2 %move.1 = (f32[64,32,128]{2,1,0:T(8,128)}, f32[64,32,128]{2,1,0:T(8,128)}, f32[64,32,128]{2,1,0:T(8,128)}) custom-call(s32[8,128]{1,0:T(8,128)S(1)} %pad.4.offsets, f32[64,32,128]{2,1,0:T(8,128)S(1)} %get-tuple-element.61.ru, f32[64,32,128]{2,1,0:T(8,128)S(1)} %get-tuple-element.62.rv, f32[64,32,128]{2,1,0:T(8,128)S(1)} %get-tuple-element.63.rp, ...), custom_call_target="tpu_custom_call" | custom-call | bytes 160000 | tf_op jit(solution)/shard_map/move/pallas_call | solution.py:393
  (1 shorter events, 0.0 us)
Async XLA Ops:
  0.6 6.1 %copy-start = (f32[64,32,128]{2,1,0:T(8,128)S(1)}, f32[64,32,128]{2,1,0:T(8,128)}, u32[]{:S(2)}) copy-start(f32[64,32,128]{2,1,0:T(8,128)} %p.9) | copy-start | bytes 3145732
  0.6 6.1 %copy-start.3 = (f32[64,32,128]{2,1,0:T(8,128)S(1)}, f32[64,32,128]{2,1,0:T(8,128)}, u32[]{:S(2)}) copy-start(f32[64,32,128]{2,1,0:T(8,128)} %v.3) | copy-start | bytes 3145732
  2.1 7.3 %copy-start.1 = (f32[64,32,128]{2,1,0:T(8,128)S(1)}, f32[64,32,128]{2,1,0:T(8,128)}, u32[]{:S(2)}) copy-start(f32[64,32,128]{2,1,0:T(8,128)} %u.5) | copy-start | bytes 3145732
  2.1 15.5 %collective-permute-start = (f32[576,128]{1,0:T(8,128)S(1)}, f32[576,128]{1,0:T(8,128)S(1)}, u32[]{:S(2)}, u32[]{:S(2)}) collective-permute-start(f32[576,128]{1,0:T(8,128)S(1)} %get-tuple-element.34), channel_id=1, source_target_pairs={{0,16},{16,0},{32,48},{48,32},{64,80},{80,64},{96,112},{112,96},{1... | collective-permute-start | bytes 884744 | tf_op jit(solution)/shard_map/ppermute | solution.py:424
  2.7 15.0 %collective-permute-start.1 = (f32[576,128]{1,0:T(8,128)S(1)}, f32[576,128]{1,0:T(8,128)S(1)}, u32[]{:S(2)}, u32[]{:S(2)}) collective-permute-start(f32[576,128]{1,0:T(8,128)S(1)} %get-tuple-element.35), channel_id=1, source_target_pairs={{0,112},{16,32},{32,16},{48,64},{64,48},{80,96},{96,80},{112,0},{1... | collective-permute-start | bytes 884744 | tf_op jit(solution)/shard_map/ppermute | solution.py:423
  7.5 2.6 %copy-start.7 = (f32[32,128]{1,0:T(8,128)S(1)}, f32[32,128]{1,0:T(8,128)}, u32[]{:S(2)}) copy-start(f32[32,128]{1,0:T(8,128)} %s_ref.1) | copy-start | bytes 49156
  7.5 3.2 %copy-start.2 = (f32[3,64,3,128]{3,1,2,0:T(8,128)S(1)}, f32[3,64,3,128]{3,1,2,0:T(8,128)}, u32[]{:S(2)}) copy-start(f32[3,64,3,128]{3,1,2,0:T(8,128)} %param.13) | copy-start | bytes 884740
  7.5 3.2 %copy-start.5 = (f32[3,64,32,3]{1,2,3,0:T(8,128)S(1)}, f32[3,64,32,3]{1,2,3,0:T(8,128)}, u32[]{:S(2)}) copy-start(f32[3,64,32,3]{1,2,3,0:T(8,128)} %param.14) | copy-start | bytes 221188
  7.5 3.2 %copy-start.6 = (f32[3,64,3,3]{1,3,2,0:T(4,128)S(1)}, f32[3,64,3,3]{1,3,2,0:T(4,128)}, u32[]{:S(2)}) copy-start(f32[3,64,3,3]{1,3,2,0:T(4,128)} %param.15) | copy-start | bytes 20740
  7.5 8.5 %copy-start.4 = (bf16[256,256]{1,0:T(8,128)(2,1)S(1)}, bf16[256,256]{1,0:T(8,128)(2,1)}, u32[]{:S(2)}) copy-start(bf16[256,256]{1,0:T(8,128)(2,1)} %constant.4.clone.rest_2_.rest_3_) | copy-start | bytes 393220
  7.5 3.8 %collective-permute-start.2 = (f32[6,32,128]{2,1,0:T(8,128)S(1)}, f32[6,32,128]{2,1,0:T(8,128)S(1)}, u32[]{:S(2)}, u32[]{:S(2)}) collective-permute-start(f32[6,32,128]{2,1,0:T(8,128)S(1)} %get-tuple-element.39), channel_id=1, source_target_pairs={{0,1},{1,0},{2,3},{3,2},{4,5},{5,4},{6,7},{7,6},{8,9},{9,8},{10,11... | collective-permute-start | bytes 294920 | tf_op jit(solution)/shard_map/ppermute | solution.py:428
  8.8 7.2 %collective-permute-start.3 = (f32[6,32,128]{2,1,0:T(8,128)S(1)}, f32[6,32,128]{2,1,0:T(8,128)S(1)}, u32[]{:S(2)}, u32[]{:S(2)}) collective-permute-start(f32[6,32,128]{2,1,0:T(8,128)S(1)} %get-tuple-element.40), channel_id=1, source_target_pairs={{0,15},{1,2},{2,1},{3,4},{4,3},{5,6},{6,5},{7,8},{8,7},{9,10},{10,... | collective-permute-start | bytes 294920 | tf_op jit(solution)/shard_map/ppermute | solution.py:429
  18.7 11.5 %collective-permute-start.4 = (f32[384,128]{1,0:T(8,128)S(1)}, f32[384,128]{1,0:T(8,128)S(1)}, u32[]{:S(2)}, u32[]{:S(2)}) collective-permute-start(f32[384,128]{1,0:T(8,128)S(1)} %get-tuple-element.46), channel_id=1, source_target_pairs={{0,16},{16,0},{32,48},{48,32},{64,80},{80,64},{96,112},{112,96},{1... | collective-permute-start | bytes 589832 | tf_op jit(solution)/shard_map/ppermute | solution.py:462
  18.8 11.4 %collective-permute-start.5 = (f32[384,128]{1,0:T(8,128)S(1)}, f32[384,128]{1,0:T(8,128)S(1)}, u32[]{:S(2)}, u32[]{:S(2)}) collective-permute-start(f32[384,128]{1,0:T(8,128)S(1)} %get-tuple-element.47), channel_id=1, source_target_pairs={{0,112},{16,32},{32,16},{48,64},{64,48},{80,96},{96,80},{112,0},{1... | collective-permute-start | bytes 589832 | tf_op jit(solution)/shard_map/ppermute | solution.py:461
  20.3 3.6 %collective-permute-start.6 = (f32[4,32,128]{2,1,0:T(8,128)S(1)}, f32[4,32,128]{2,1,0:T(8,128)S(1)}, u32[]{:S(2)}, u32[]{:S(2)}) collective-permute-start(f32[4,32,128]{2,1,0:T(8,128)S(1)} %get-tuple-element.53), channel_id=1, source_target_pairs={{0,1},{1,0},{2,3},{3,2},{4,5},{5,4},{6,7},{7,6},{8,9},{9,8},{10,11... | collective-permute-start | bytes 196616 | tf_op jit(solution)/shard_map/ppermute | solution.py:466
  22.7 5.9 %collective-permute-start.7 = (f32[4,32,128]{2,1,0:T(8,128)S(1)}, f32[4,32,128]{2,1,0:T(8,128)S(1)}, u32[]{:S(2)}, u32[]{:S(2)}) collective-permute-start(f32[4,32,128]{2,1,0:T(8,128)S(1)} %get-tuple-element.54), channel_id=1, source_target_pairs={{0,15},{1,2},{2,1},{3,4},{4,3},{5,6},{6,5},{7,8},{8,7},{9,10},{10,... | collective-permute-start | bytes 196616 | tf_op jit(solution)/shard_map/ppermute | solution.py:467
  31.1 12.1 %collective-permute-start.8 = (f32[384,128]{1,0:T(8,128)S(1)}, f32[384,128]{1,0:T(8,128)S(1)}, u32[]{:S(2)}, u32[]{:S(2)}) collective-permute-start(f32[384,128]{1,0:T(8,128)S(1)} %get-tuple-element.64), channel_id=1, source_target_pairs={{0,112},{16,0},{32,16},{48,32},{64,48},{80,64},{96,80},{112,96},{1... | collective-permute-start | bytes 589832 | tf_op jit(solution)/shard_map/ppermute | solution.py:490
  31.5 1.0 %copy-start.8 = (s32[2]{0:T(128)S(1)}, s32[2]{0:T(128)}, u32[]{:S(2)}) copy-start(s32[2]{0:T(128)} %param.16) | copy-start | bytes 28
  32.3 10.9 %collective-permute-start.9 = (f32[8,32,128]{2,1,0:T(8,128)S(1)}, f32[8,32,128]{2,1,0:T(8,128)S(1)}, u32[]{:S(2)}, u32[]{:S(2)}) collective-permute-start(f32[8,32,128]{2,1,0:T(8,128)S(1)} %north_pack.1), channel_id=1, source_target_pairs={{0,15},{1,0},{2,1},{3,2},{4,3},{5,4},{6,5},{7,6},{8,7},{9,8},{10,9... | collective-permute-start | bytes 393224 | tf_op jit(solution)/shard_map/ppermute | solution.py:498
  32.4 10.8 %collective-permute-start.10 = (f32[8,8,128]{2,1,0:T(8,128)S(1)}, f32[8,8,128]{2,1,0:T(8,128)S(1)}, u32[]{:S(2)}, u32[]{:S(2)}) collective-permute-start(f32[8,8,128]{2,1,0:T(8,128)S(1)} %corner_pack.1.after), channel_id=1, source_target_pairs={{0,127},{1,112},{2,113},{3,114},{4,115},{5,116},{6,117},{7,118},{8... | collective-permute-start | bytes 98312 | tf_op jit(solution)/shard_map/ppermute | solution.py:494

commit v4 on v3

--- a/solution.py
+++ b/solution.py
@@ -150,9 +150,9 @@
 
 def inner_kernel(first_step, p, v, ex, *rest):
     if first_step:
-        inv, g, mat, y1, y2, keep1, keep2, keep3, p_out, v_out, vh_out, rest_out, w_buf = rest
+        inv, g, mat, y2, y1, keep1, keep2, keep3, p_out, v_out, vh_out, rest_out, w_buf = rest
     else:
-        vh_in, inv, g, mat, y1, y2, p_out, v_out, rest_out, w_buf = rest
+        vh_in, inv, g, mat, y2, y1, p_out, v_out, rest_out, w_buf = rest
     lanes = lane_index()
     gy = lax.axis_index("gy")
     even_y = gy % 2 == 0
@@ -444,7 +444,7 @@
     p1, v1, vh1, rest = call(
         functools.partial(inner_kernel, True),
         (field, field, field, outer),
-        (pressure, wind_north, ex, inv, g, mat, y1, y2, pe_strip, pn_strip, pe),
+        (pressure, wind_north, ex, inv, g, mat, y2, y1, pe_strip, pn_strip, pe),
         buffers((64, 16, 128)),
         name="inner1",
         specs={8: ANY, 9: ANY, 10: ANY},
@@ -471,7 +471,7 @@
     p2, v2, rest = call(
         functools.partial(inner_kernel, False),
         (field, field, outer),
-        (p1, v1, ex, vh1, inv, g, mat, y1, y2),
+        (p1, v1, ex, vh1, inv, g, mat, y2, y1),
         buffers((64, 16, 128)),
         name="inner2",
         us=0.3,

time: 45.9 us -> 44.6 us (0.972)
  the two profiles are of different devices: /device:TPU:31 before, /device:TPU:7 now
where the time goes in v4:
time: 44.6 us; the launch traced here: 44.5 us
  starting transfers between devices  17.5 us (39%)
  Pallas kernels  14.6 us (33%)
  waiting for transfers between devices  11.6 us (26%)
  between operations  0.87 us (2%)
    pallas_call x15, Pallas kernels, call(): pl.pallas_call(body, out_shape=out_shape, in_specs=[specs.get(k, VMEM) fo...  14.6 us
    ppermute x2, starting transfers between devices, on_device(): x2 = lax.ppermute(second, 'gx', x_out)  7.52 us
    ppermute x2, waiting for transfers between devices, on_device(): y2 = lax.ppermute(second, 'gy', y_out)  6.46 us
    ppermute x1, waiting for transfers between devices, on_device(): from_corner = lax.ppermute(corner, ('gx', 'gy'), down)  5.08 us
    ppermute x2, starting transfers between devices, on_device(): y2 = lax.ppermute(second, 'gy', y_out)  4.91 us
    ppermute x1, starting transfers between devices, on_device(): east = lax.ppermute(east, 'gx', down_x)  2.92 us
    ppermute x2, starting transfers between devices, on_device(): x1 = lax.ppermute(first, 'gx', x_in)  1.46 us
  transfers between devices with their start and end apart: 11, of which 3 were waited for; matrix products, arithmetic and copies ran while one was open for 0% of the time, Pallas kernels for 20%

profile of v4, /device:TPU:7, one launch (start us, length us, event | category | flops | bytes accessed | tf_op | source)
XLA Modules:
  0.0 44.5 jit_solution(10218295303927996619)
XLA Ops:
  0.6 0.0 copy-start
  0.6 0.0 copy-start.3
  0.7 1.5 %x_edges.1 = (f32[576,128]{1,0:T(8,128)S(1)}, f32[576,128]{1,0:T(8,128)S(1)}) custom-call(f32[64,32,128]{2,1,0:T(8,128)} %p.9, f32[64,32,128]{2,1,0:T(8,128)} %u.5), custom_call_target="tpu_custom_call" | custom-call | bytes 160000 | tf_op jit(solution)/shard_map/x_edges/pallas_call | solution.py:393
  2.1 0.0 copy-start.1
  2.1 1.4 %collective-permute-start = (f32[576,128]{1,0:T(8,128)S(1)}, f32[576,128]{1,0:T(8,128)S(1)}, u32[]{:S(2)}, u32[]{:S(2)}) collective-permute-start(f32[576,128]{1,0:T(8,128)S(1)} %get-tuple-element.34), channel_id=1, source_target_pairs={{0,16},{16,0},{32,48},{48,32},{64,80},{80,64},{96,112},{112,96},{1... | collective-permute-start | bytes 884744 | tf_op jit(solution)/shard_map/ppermute | solution.py:424
  3.5 5.2 %collective-permute-start.1 = (f32[576,128]{1,0:T(8,128)S(1)}, f32[576,128]{1,0:T(8,128)S(1)}, u32[]{:S(2)}, u32[]{:S(2)}) collective-permute-start(f32[576,128]{1,0:T(8,128)S(1)} %get-tuple-element.35), channel_id=1, source_target_pairs={{0,112},{16,32},{32,16},{48,64},{64,48},{80,96},{96,80},{112,0},{1... | collective-permute-start | bytes 884744 | tf_op jit(solution)/shard_map/ppermute | solution.py:423
  8.7 0.0 copy-done
  8.7 0.0 copy-done.3
  8.7 0.7 %y_edges.1 = (f32[6,32,128]{2,1,0:T(8,128)S(1)}, f32[6,32,128]{2,1,0:T(8,128)S(1)}) custom-call(f32[64,32,128]{2,1,0:T(8,128)S(1)} %copy-done, f32[64,32,128]{2,1,0:T(8,128)S(1)} %copy-done.3), custom_call_target="tpu_custom_call" | custom-call | bytes 160000 | tf_op jit(solution)/shard_map/y_edges/pallas_call | solution.py:393
  9.4 0.0 copy-start.7
  9.4 0.0 copy-start.2
  9.4 0.0 copy-start.5
  9.4 0.0 copy-start.6
  9.5 0.0 copy-start.4
  9.5 1.9 %collective-permute-start.2 = (f32[6,32,128]{2,1,0:T(8,128)S(1)}, f32[6,32,128]{2,1,0:T(8,128)S(1)}, u32[]{:S(2)}, u32[]{:S(2)}) collective-permute-start(f32[6,32,128]{2,1,0:T(8,128)S(1)} %get-tuple-element.39), channel_id=1, source_target_pairs={{0,15},{1,2},{2,1},{3,4},{4,3},{5,6},{6,5},{7,8},{8,7},{9,10},{10,... | collective-permute-start | bytes 294920 | tf_op jit(solution)/shard_map/ppermute | solution.py:429
  11.3 0.0 collective-permute-start.3
  11.3 0.0 copy-done.1
  11.3 0.6 %across1.1 = (f32[64,48,128]{2,1,0:T(8,128)S(1)}, f32[64,16,128]{2,1,0:T(8,128)S(1)}) custom-call(f32[64,32,128]{2,1,0:T(8,128)S(1)} %copy-done, f32[64,32,128]{2,1,0:T(8,128)S(1)} %copy-done.1), custom_call_target="tpu_custom_call" | custom-call | bytes 160000 | tf_op jit(solution)/shard_map/across1/pallas_call | solution.py:393
  11.9 0.0 copy-done.7
  11.9 0.6 %coefficients.1 = (f32[64,32,128]{2,1,0:T(8,128)S(1)}, f32[64,32,128]{2,1,0:T(8,128)S(1)}) custom-call(f32[32,128]{1,0:T(8,128)S(1)} %copy-done.7), custom_call_target="tpu_custom_call" | custom-call | bytes 160000 | tf_op jit(solution)/shard_map/coefficients/pallas_call | solution.py:393
  12.5 0.0 copy-done.2
  12.5 0.0 copy-done.5
  12.5 0.0 copy-done.6
  12.5 0.7 %parents.1 = (f32[8,8,128]{2,1,0:T(8,128)S(1)}, f32[8,40,128]{2,1,0:T(8,128)S(1)}) custom-call(f32[3,3,64,128]{3,2,1,0:T(8,128)S(1)} %bitcast.4, f32[3,3,32,64]{3,2,1,0:T(8,128)S(1)} %bitcast.8, f32[3,3,3,64]{3,2,1,0:T(4,128)S(1)} %bitcast.9), custom_call_target="tpu_custom_call" | custom-call | bytes 160000 | tf_op jit(solution)/shard_map/parents/pallas_call | solution.py:393
  13.2 3.5 %collective-permute-done.2.rest_3_ = f32[6,32,128]{2,1,0:T(8,128)S(1)} collective-permute-done((f32[6,32,128]{2,1,0:T(8,128)S(1)}, f32[6,32,128]{2,1,0:T(8,128)S(1)}, u32[]{:S(2)}, u32[]{:S(2)}) %collective-permute-start.2) | collective-permute-done | bytes 98336 | tf_op jit(solution)/shard_map/ppermute | solution.py:429
  16.8 0.0 collective-permute-done.3.rest_4_
  16.8 0.0 copy-done.4
  16.8 1.6 %inner1.1 = (f32[64,32,128]{2,1,0:T(8,128)S(1)}, f32[64,32,128]{2,1,0:T(8,128)S(1)}, f32[64,32,128]{2,1,0:T(8,128)S(1)}, f32[64,16,128]{2,1,0:T(8,128)S(1)}) custom-call(f32[64,32,128]{2,1,0:T(8,128)S(1)} %copy-done, f32[64,32,128]{2,1,0:T(8,128)S(1)} %copy-done.3, f32[64,16,128]{2,1,0:T(8,128)S(1)} %get-tuple-element.38.ex, ...), custom_call_target="tpu_custom_call" | custom-call | bytes 960000 | tf_op jit(solution)/shard_map/inner1/pallas_call | solution.py:393
  18.4 0.0 collective-permute-done.x1
  18.4 0.0 collective-permute-done.1.x2
  18.4 1.0 %outer1.1 = (f32[64,32,128]{2,1,0:T(8,128)S(1)}, f32[64,48,128]{2,1,0:T(8,128)S(1)}, f32[384,128]{1,0:T(8,128)S(1)}, f32[384,128]{1,0:T(8,128)S(1)}) custom-call(f32[576,128]{1,0:T(8,128)S(1)} %collective-permute-done.x1, f32[576,128]{1,0:T(8,128)S(1)} %collective-permute-done.1.x2, ...), custom_call_target="tpu_custom_call", output_to_operand_aliasing={{0}: (7, {}), {1}: (8, {})} | custom-call | bytes 160000 | tf_op jit(solution)/shard_map/outer1/pallas_call | solution.py:393
  19.4 0.1 collective-permute-start.4
  19.5 2.3 %collective-permute-start.5 = (f32[384,128]{1,0:T(8,128)S(1)}, f32[384,128]{1,0:T(8,128)S(1)}, u32[]{:S(2)}, u32[]{:S(2)}) collective-permute-start(f32[384,128]{1,0:T(8,128)S(1)} %get-tuple-element.47), channel_id=1, source_target_pairs={{0,112},{16,32},{32,16},{48,64},{64,48},{80,96},{96,80},{112,0},{1... | collective-permute-start | bytes 589832 | tf_op jit(solution)/shard_map/ppermute | solution.py:461
  21.8 0.3 y_pack.1
  22.1 3.1 %collective-permute-start.6 = (f32[4,32,128]{2,1,0:T(8,128)S(1)}, f32[4,32,128]{2,1,0:T(8,128)S(1)}, u32[]{:S(2)}, u32[]{:S(2)}) collective-permute-start(f32[4,32,128]{2,1,0:T(8,128)S(1)} %get-tuple-element.53), channel_id=1, source_target_pairs={{0,15},{1,2},{2,1},{3,4},{4,3},{5,6},{6,5},{7,8},{8,7},{9,10},{10,... | collective-permute-start | bytes 196616 | tf_op jit(solution)/shard_map/ppermute | solution.py:467
  25.2 0.0 collective-permute-start.7
  25.2 0.6 %across2.1 = (f32[64,48,128]{2,1,0:T(8,128)S(1)}, f32[64,16,128]{2,1,0:T(8,128)S(1)}) custom-call(f32[64,32,128]{2,1,0:T(8,128)S(1)} %get-tuple-element.48.p, f32[64,48,128]{2,1,0:T(8,128)S(1)} %get-tuple-element.49.u), custom_call_target="tpu_custom_call" | custom-call | bytes 160000 | tf_op jit(solution)/shard_map/across2/pallas_call | solution.py:393
  25.8 2.9 %collective-permute-done.6.rest_4_ = f32[4,32,128]{2,1,0:T(8,128)S(1)} collective-permute-done((f32[4,32,128]{2,1,0:T(8,128)S(1)}, f32[4,32,128]{2,1,0:T(8,128)S(1)}, u32[]{:S(2)}, u32[]{:S(2)}) %collective-permute-start.6) | collective-permute-done | bytes 65568 | tf_op jit(solution)/shard_map/ppermute | solution.py:467
  28.7 0.0 collective-permute-done.7.rest_5_
  28.7 1.6 %inner2.1 = (f32[64,32,128]{2,1,0:T(8,128)S(1)}, f32[64,32,128]{2,1,0:T(8,128)S(1)}, f32[64,16,128]{2,1,0:T(8,128)S(1)}) custom-call(f32[64,32,128]{2,1,0:T(8,128)S(1)} %get-tuple-element.48.p, f32[64,32,128]{2,1,0:T(8,128)S(1)} %get-tuple-element.50.v, f32[64,16,128]{2,1,0:T(8,128)S(1)} %get-tuple-element.51.ex, ...), custom_call_target="tpu_custom_call" | custom-call | bytes 960000 | tf_op jit(solution)/shard_map/inner2/pallas_call | solution.py:393
  30.4 0.0 collective-permute-done.4.x1
  30.4 0.0 collective-permute-done.5.x2
  30.4 0.9 %outer2.1 = (f32[64,32,128]{2,1,0:T(8,128)S(1)}, f32[64,48,128]{2,1,0:T(8,128)S(1)}, f32[384,128]{1,0:T(8,128)S(1)}) custom-call(f32[384,128]{1,0:T(8,128)S(1)} %collective-permute-done.4.x1, f32[384,128]{1,0:T(8,128)S(1)} %collective-permute-done.5.x2, f32[64,32,128]{2,1,0:T(8,128)S(1)} %get-tuple-element.48.p, ...), custom_call_target="tpu_custom_call", output_to_operand_aliasing={{0}: (7, {}), {1}: (8, {})} | custom-call | bytes 160000 | tf_op jit(solution)/shard_map/outer2/pallas_call | solution.py:393
  31.3 2.9 %collective-permute-start.8 = (f32[384,128]{1,0:T(8,128)S(1)}, f32[384,128]{1,0:T(8,128)S(1)}, u32[]{:S(2)}, u32[]{:S(2)}) collective-permute-start(f32[384,128]{1,0:T(8,128)S(1)} %get-tuple-element.64), channel_id=1, source_target_pairs={{0,112},{16,0},{32,16},{48,32},{64,48},{80,64},{96,80},{112,96},{1... | collective-permute-start | bytes 589832 | tf_op jit(solution)/shard_map/ppermute | solution.py:490
  34.2 0.3 corner_pack.1.after
  34.5 0.0 copy-start.8
  34.5 0.8 %north_pack.1 = f32[8,32,128]{2,1,0:T(8,128)S(1)} custom-call(f32[64,48,128]{2,1,0:T(8,128)S(1)} %get-tuple-element.59.u, f32[64,32,128]{2,1,0:T(8,128)S(1)} %get-tuple-element.58.tail_0_.v, f32[64,32,128]{2,1,0:T(8,128)S(1)} %get-tuple-element.60.p, f32[8,40,128]{2,1,0:T(8,128)S(1)} %get-tuple-element.42.rest_6_.pn, f32[8,8,128]{2,1,0:T(8,128)S(1)} %corner_pack.1.after), custom_call_target="tpu_custom_call" | custom-call | bytes 160000 | tf_op jit(solution)/shard_map/north_pack/pallas_call | solution.py:393
  35.3 0.7 %collective-permute-start.9 = (f32[8,32,128]{2,1,0:T(8,128)S(1)}, f32[8,32,128]{2,1,0:T(8,128)S(1)}, u32[]{:S(2)}, u32[]{:S(2)}) collective-permute-start(f32[8,32,128]{2,1,0:T(8,128)S(1)} %north_pack.1), channel_id=1, source_target_pairs={{0,15},{1,0},{2,1},{3,2},{4,3},{5,4},{6,5},{7,6},{8,7},{9,8},{10,9... | collective-permute-start | bytes 393224 | tf_op jit(solution)/shard_map/ppermute | solution.py:498
  36.0 0.0 collective-permute-start.10
  36.0 0.0 copy-done.8
  36.0 1.2 %turn.1 = (f32[64,32,128]{2,1,0:T(8,128)S(1)}, f32[64,32,128]{2,1,0:T(8,128)S(1)}, f32[64,32,128]{2,1,0:T(8,128)S(1)}) custom-call(s32[8,128]{1,0:T(8,128)S(1)} %pad.4.offsets, f32[64,48,128]{2,1,0:T(8,128)S(1)} %get-tuple-element.59.u, f32[64,32,128]{2,1,0:T(8,128)S(1)} %get-tuple-element.58.tail_0_.v, f32[64,32,128]{2,1,0:T(8,128)S(1)} %get-tuple-element.60.p, ...), custom_call_target="tpu_custom_call" | custom-call | bytes 160000 | tf_op jit(solution)/shard_map/turn/pallas_call | solution.py:393
  37.3 5.1 %collective-permute-done.10.corner = f32[8,8,128]{2,1,0:T(8,128)S(1)} collective-permute-done((f32[8,8,128]{2,1,0:T(8,128)S(1)}, f32[8,8,128]{2,1,0:T(8,128)S(1)}, u32[]{:S(2)}, u32[]{:S(2)}) %collective-permute-start.10) | collective-permute-done | bytes 32800 | tf_op jit(solution)/shard_map/ppermute | solution.py:494
  42.3 0.0 collective-permute-done.9.north
  42.3 0.0 collective-permute-done.8.east
  42.3 2.2 %move.1 = (f32[64,32,128]{2,1,0:T(8,128)}, f32[64,32,128]{2,1,0:T(8,128)}, f32[64,32,128]{2,1,0:T(8,128)}) custom-call(s32[8,128]{1,0:T(8,128)S(1)} %pad.4.offsets, f32[64,32,128]{2,1,0:T(8,128)S(1)} %get-tuple-element.61.ru, f32[64,32,128]{2,1,0:T(8,128)S(1)} %get-tuple-element.62.rv, f32[64,32,128]{2,1,0:T(8,128)S(1)} %get-tuple-element.63.rp, ...), custom_call_target="tpu_custom_call" | custom-call | bytes 160000 | tf_op jit(solution)/shard_map/move/pallas_call | solution.py:393
  (1 shorter events, 0.0 us)
Async XLA Ops:
  0.6 8.1 %copy-start = (f32[64,32,128]{2,1,0:T(8,128)S(1)}, f32[64,32,128]{2,1,0:T(8,128)}, u32[]{:S(2)}) copy-start(f32[64,32,128]{2,1,0:T(8,128)} %p.9) | copy-start | bytes 3145732
  0.6 8.1 %copy-start.3 = (f32[64,32,128]{2,1,0:T(8,128)S(1)}, f32[64,32,128]{2,1,0:T(8,128)}, u32[]{:S(2)}) copy-start(f32[64,32,128]{2,1,0:T(8,128)} %v.3) | copy-start | bytes 3145732
  2.1 9.2 %copy-start.1 = (f32[64,32,128]{2,1,0:T(8,128)S(1)}, f32[64,32,128]{2,1,0:T(8,128)}, u32[]{:S(2)}) copy-start(f32[64,32,128]{2,1,0:T(8,128)} %u.5) | copy-start | bytes 3145732
  2.1 16.3 %collective-permute-start = (f32[576,128]{1,0:T(8,128)S(1)}, f32[576,128]{1,0:T(8,128)S(1)}, u32[]{:S(2)}, u32[]{:S(2)}) collective-permute-start(f32[576,128]{1,0:T(8,128)S(1)} %get-tuple-element.34), channel_id=1, source_target_pairs={{0,16},{16,0},{32,48},{48,32},{64,80},{80,64},{96,112},{112,96},{1... | collective-permute-start | bytes 884744 | tf_op jit(solution)/shard_map/ppermute | solution.py:424
  3.5 14.9 %collective-permute-start.1 = (f32[576,128]{1,0:T(8,128)S(1)}, f32[576,128]{1,0:T(8,128)S(1)}, u32[]{:S(2)}, u32[]{:S(2)}) collective-permute-start(f32[576,128]{1,0:T(8,128)S(1)} %get-tuple-element.35), channel_id=1, source_target_pairs={{0,112},{16,32},{32,16},{48,64},{64,48},{80,96},{96,80},{112,0},{1... | collective-permute-start | bytes 884744 | tf_op jit(solution)/shard_map/ppermute | solution.py:423
  9.4 2.5 %copy-start.7 = (f32[32,128]{1,0:T(8,128)S(1)}, f32[32,128]{1,0:T(8,128)}, u32[]{:S(2)}) copy-start(f32[32,128]{1,0:T(8,128)} %s_ref.1) | copy-start | bytes 49156
  9.4 3.1 %copy-start.2 = (f32[3,64,3,128]{3,1,2,0:T(8,128)S(1)}, f32[3,64,3,128]{3,1,2,0:T(8,128)}, u32[]{:S(2)}) copy-start(f32[3,64,3,128]{3,1,2,0:T(8,128)} %param.13) | copy-start | bytes 884740
  9.4 3.1 %copy-start.5 = (f32[3,64,32,3]{1,2,3,0:T(8,128)S(1)}, f32[3,64,32,3]{1,2,3,0:T(8,128)}, u32[]{:S(2)}) copy-start(f32[3,64,32,3]{1,2,3,0:T(8,128)} %param.14) | copy-start | bytes 221188
  9.4 3.1 %copy-start.6 = (f32[3,64,3,3]{1,3,2,0:T(4,128)S(1)}, f32[3,64,3,3]{1,3,2,0:T(4,128)}, u32[]{:S(2)}) copy-start(f32[3,64,3,3]{1,3,2,0:T(4,128)} %param.15) | copy-start | bytes 20740
  9.5 7.3 %copy-start.4 = (bf16[256,256]{1,0:T(8,128)(2,1)S(1)}, bf16[256,256]{1,0:T(8,128)(2,1)}, u32[]{:S(2)}) copy-start(bf16[256,256]{1,0:T(8,128)(2,1)} %constant.4.clone.rest_2_.rest_3_) | copy-start | bytes 393220
  9.5 7.3 %collective-permute-start.2 = (f32[6,32,128]{2,1,0:T(8,128)S(1)}, f32[6,32,128]{2,1,0:T(8,128)S(1)}, u32[]{:S(2)}, u32[]{:S(2)}) collective-permute-start(f32[6,32,128]{2,1,0:T(8,128)S(1)} %get-tuple-element.39), channel_id=1, source_target_pairs={{0,15},{1,2},{2,1},{3,4},{4,3},{5,6},{6,5},{7,8},{8,7},{9,10},{10,... | collective-permute-start | bytes 294920 | tf_op jit(solution)/shard_map/ppermute | solution.py:429
  11.3 5.4 %collective-permute-start.3 = (f32[6,32,128]{2,1,0:T(8,128)S(1)}, f32[6,32,128]{2,1,0:T(8,128)S(1)}, u32[]{:S(2)}, u32[]{:S(2)}) collective-permute-start(f32[6,32,128]{2,1,0:T(8,128)S(1)} %get-tuple-element.40), channel_id=1, source_target_pairs={{0,1},{1,0},{2,3},{3,2},{4,5},{5,4},{6,7},{7,6},{8,9},{9,8},{10,11... | collective-permute-start | bytes 294920 | tf_op jit(solution)/shard_map/ppermute | solution.py:428
  19.4 11.0 %collective-permute-start.4 = (f32[384,128]{1,0:T(8,128)S(1)}, f32[384,128]{1,0:T(8,128)S(1)}, u32[]{:S(2)}, u32[]{:S(2)}) collective-permute-start(f32[384,128]{1,0:T(8,128)S(1)} %get-tuple-element.46), channel_id=1, source_target_pairs={{0,16},{16,0},{32,48},{48,32},{64,80},{80,64},{96,112},{112,96},{1... | collective-permute-start | bytes 589832 | tf_op jit(solution)/shard_map/ppermute | solution.py:462
  19.5 10.9 %collective-permute-start.5 = (f32[384,128]{1,0:T(8,128)S(1)}, f32[384,128]{1,0:T(8,128)S(1)}, u32[]{:S(2)}, u32[]{:S(2)}) collective-permute-start(f32[384,128]{1,0:T(8,128)S(1)} %get-tuple-element.47), channel_id=1, source_target_pairs={{0,112},{16,32},{32,16},{48,64},{64,48},{80,96},{96,80},{112,0},{1... | collective-permute-start | bytes 589832 | tf_op jit(solution)/shard_map/ppermute | solution.py:461
  22.1 6.6 %collective-permute-start.6 = (f32[4,32,128]{2,1,0:T(8,128)S(1)}, f32[4,32,128]{2,1,0:T(8,128)S(1)}, u32[]{:S(2)}, u32[]{:S(2)}) collective-permute-start(f32[4,32,128]{2,1,0:T(8,128)S(1)} %get-tuple-element.53), channel_id=1, source_target_pairs={{0,15},{1,2},{2,1},{3,4},{4,3},{5,6},{6,5},{7,8},{8,7},{9,10},{10,... | collective-permute-start | bytes 196616 | tf_op jit(solution)/shard_map/ppermute | solution.py:467
  25.2 3.5 %collective-permute-start.7 = (f32[4,32,128]{2,1,0:T(8,128)S(1)}, f32[4,32,128]{2,1,0:T(8,128)S(1)}, u32[]{:S(2)}, u32[]{:S(2)}) collective-permute-start(f32[4,32,128]{2,1,0:T(8,128)S(1)} %get-tuple-element.54), channel_id=1, source_target_pairs={{0,1},{1,0},{2,3},{3,2},{4,5},{5,4},{6,7},{7,6},{8,9},{9,8},{10,11... | collective-permute-start | bytes 196616 | tf_op jit(solution)/shard_map/ppermute | solution.py:466
  31.3 11.1 %collective-permute-start.8 = (f32[384,128]{1,0:T(8,128)S(1)}, f32[384,128]{1,0:T(8,128)S(1)}, u32[]{:S(2)}, u32[]{:S(2)}) collective-permute-start(f32[384,128]{1,0:T(8,128)S(1)} %get-tuple-element.64), channel_id=1, source_target_pairs={{0,112},{16,0},{32,16},{48,32},{64,48},{80,64},{96,80},{112,96},{1... | collective-permute-start | bytes 589832 | tf_op jit(solution)/shard_map/ppermute | solution.py:490
  34.5 1.5 %copy-start.8 = (s32[2]{0:T(128)S(1)}, s32[2]{0:T(128)}, u32[]{:S(2)}) copy-start(s32[2]{0:T(128)} %param.16) | copy-start | bytes 28
  35.3 7.0 %collective-permute-start.9 = (f32[8,32,128]{2,1,0:T(8,128)S(1)}, f32[8,32,128]{2,1,0:T(8,128)S(1)}, u32[]{:S(2)}, u32[]{:S(2)}) collective-permute-start(f32[8,32,128]{2,1,0:T(8,128)S(1)} %north_pack.1), channel_id=1, source_target_pairs={{0,15},{1,0},{2,1},{3,2},{4,3},{5,4},{6,5},{7,6},{8,7},{9,8},{10,9... | collective-permute-start | bytes 393224 | tf_op jit(solution)/shard_map/ppermute | solution.py:498
  36.0 6.3 %collective-permute-start.10 = (f32[8,8,128]{2,1,0:T(8,128)S(1)}, f32[8,8,128]{2,1,0:T(8,128)S(1)}, u32[]{:S(2)}, u32[]{:S(2)}) collective-permute-start(f32[8,8,128]{2,1,0:T(8,128)S(1)} %corner_pack.1.after), channel_id=1, source_target_pairs={{0,127},{1,112},{2,113},{3,114},{4,115},{5,116},{6,117},{7,118},{8... | collective-permute-start | bytes 98312 | tf_op jit(solution)/shard_map/ppermute | solution.py:494
